TPU v7x, 128 devices: a whole 4x4x4 slice. The times are simulated.
128 devices in a mesh: grp: 4 (over y_lo, core), dp: 32 (over x, y_hi, z).
Axes of the slice: x: 4, y: 4 (y_hi: 2, y_lo: 2; y = y_hi * 2 + y_lo), z: 4, core: 2. Of those that a mesh axis runs over, the one named last changes fastest.
Arguments:
- student: bfloat16 [64, 32, 32, 1280], P('dp', 'grp'), may hold values from -6 to 6
- dino_feat: bfloat16 [64, 36, 36, 1536], P('dp', None, None, 'grp'), may hold values from -6 to 6
- siglip_feat: bfloat16 [64, 36, 36, 1152], P('dp', None, None, 'grp'), may hold values from -6 to 6
- sam_feat: bfloat16 [64, 32, 32, 1280], P('dp', None, None, 'grp'), may hold values from -6 to 6
- w1_dino: bfloat16 [1280, 1536], replicated, may hold values from -0.15625 to 0.15625
- w2_dino: bfloat16 [1536, 1536], P(None, 'grp'), may hold values from -0.15625 to 0.15625
- w1_siglip: bfloat16 [1280, 1152], replicated, may hold values from -0.15625 to 0.15625
- w2_siglip: bfloat16 [1152, 1152], P(None, 'grp'), may hold values from -0.1875 to 0.1875
- w1_sam: bfloat16 [1280, 1280], replicated, may hold values from -0.15625 to 0.15625
- w2_sam: bfloat16 [1280, 1280], P(None, 'grp'), may hold values from -0.15625 to 0.15625
Outputs:
- grad_dino: float32 [1536, 1536], P('dp', 'grp')
- grad_siglip: float32 [1152, 1152], P('dp', 'grp')
- grad_sam: float32 [1280, 1280], P('dp', 'grp')
All inputs are finite; a program needn't handle non-finite values.
Results may differ from a plain program's by a relative error of at most 0.012.
Values may be sent and summed in bfloat16 or wider, within the bound.
No kernel may reach another device: no remote copies, remote signals or barrier semaphores. Data moves between devices by JAX's collectives and lax.ppermute only.
A program may use at most 128 MiB of HBM per device.

v0:
```python
import functools
import math

import jax
import jax.numpy as jnp
from jax import lax
from jax.experimental import pallas as pl
from jax.experimental.pallas import tpu as pltpu
from jax.sharding import PartitionSpec as P

epsilon = 1e-06

f32 = jnp.float32
bf16 = jnp.bfloat16

CORE = [(g, g ^ 1) for g in range(4)]
CHIP = [(g, g ^ 2) for g in range(4)]

HALF = 384
MIB = 1024 * 1024


def pad_lanes(x):
    rows, width = x.shape
    if width == HALF:
        return x
    return jnp.concatenate([x, jnp.zeros((rows, HALF - width), x.dtype)], axis=1)


def resample_into(out_ref, at, feat_ref):
    _, in_rows, in_cols, width = feat_ref.shape
    out_rows = in_rows * 8 // 9
    slot = lax.broadcasted_iota(jnp.int32, (8, 1), 0).astype(f32)
    right = 0.125 * slot + 0.0625
    for r in range(out_rows):
        weight = 0.125 * (r % 8) + 0.0625
        first = r // 8 * 9 + r % 8
        row = (1.0 - weight) * feat_ref[0, first].astype(f32) + weight * feat_ref[
            0, first + 1
        ].astype(f32)
        blocks = []
        for b in range(in_cols // 9):
            blocks.append(
                (1.0 - right) * row[9 * b : 9 * b + 8] + right * row[9 * b + 1 : 9 * b + 9]
            )
        done = pad_lanes(jnp.concatenate(blocks, axis=0)).astype(bf16)
        count = done.shape[0]
        out_ref[0, 0, r * count : (r + 1) * count, at * HALF : (at + 1) * HALF] = done


def targets_kernel(order_ref, dino, siglip, sam, kept, sent):
    def fill(out):
        resample_into(out, 0, dino)
        resample_into(out, 2, siglip)
        _, rows, cols, width = sam.shape
        out[0, 0, :, HALF : 2 * HALF] = pad_lanes(sam[0].reshape(rows * cols, width))

    slot = pl.program_id(0)

    @pl.when(slot < 2)
    def _():
        fill(sent)

    @pl.when(slot >= 2)
    def _():
        fill(kept)


def targets(order, dino, siglip, sam):
    n = sam.shape[0]
    run = sam.shape[1] // 4 * sam.shape[2]

    def block_of(feat):
        rows = feat.shape[1] // 4
        return pl.BlockSpec(
            (1, rows) + feat.shape[2:], lambda s, i, order: (i, order[s], 0, 0)
        )

    sent = pl.BlockSpec(
        (1, 1, run, 3 * HALF),
        lambda s, i, order: (jnp.minimum(s, 1), jnp.where(s < 2, i, n - 1), 0, 0),
    )
    kept = pl.BlockSpec(
        (1, 1, run, 3 * HALF),
        lambda s, i, order: (jnp.maximum(s, 2) - 2, jnp.where(s < 2, 0, i), 0, 0),
    )
    outs = pl.pallas_call(
        targets_kernel,
        grid_spec=pltpu.PrefetchScalarGridSpec(
            num_scalar_prefetch=1,
            grid=(4, n),
            in_specs=[block_of(dino), block_of(siglip), block_of(sam)],
            out_specs=[kept, sent],
        ),
        out_shape=[jax.ShapeDtypeStruct((2, n, run, 3 * HALF), bf16)] * 2,
        compiler_params=pltpu.CompilerParams(vmem_limit_bytes=12 * MIB),
        cost_estimate=pl.CostEstimate(flops=1000, bytes_accessed=1000, transcendentals=0),
        name="targets",
    )(order, dino, siglip, sam)
    return [o.reshape(2 * n * run, 3 * HALF) for o in outs]


def gelu(x):
    inner = x * (0.7978845608028654 + (0.7978845608028654 * 0.044715) * (x * x))
    half = 0.5 * x
    return half + half * jnp.tanh(inner)


def copies_of(refs, n):
    return refs[:n], refs[n:]


def adapt_kernel(which, fresh, turned, slots, pieces, *refs):
    teachers = len(turned)
    x_in, refs = copies_of(refs, pieces)
    (goal_o_in, goal_s_in), refs = copies_of(refs, 2)
    ins, refs = copies_of(refs, 3 * teachers)
    if not fresh:
        refs = refs[4 * teachers :]
    outs, refs = copies_of(refs, 4 * teachers)
    x, refs = refs[0], refs[1:]
    bufs, refs = copies_of(refs, 6 * teachers)
    in_sem, out_sem = refs
    rows = x.shape[0]
    part = 256
    at_out = pl.ds(which * rows, rows)

    tokens = []
    for i, piece in enumerate(x_in):
        at = sum(p.shape[0] for p in x_in[:i])
        copy = pltpu.make_async_copy(
            piece, x.at[pl.ds(at, piece.shape[0])], in_sem.at[5 * teachers + i]
        )
        copy.start()
        tokens.append(copy)
    loads = []
    for t in range(teachers):
        w1_in, w2o_in, w2s_in = ins[3 * t : 3 * t + 3]
        lanes = pl.ds(slots[t] * HALF, HALF)
        w1, w2, goal = bufs[6 * t : 6 * t + 3]
        if turned[t]:
            width = w2o_in.shape[0]
            w2o, w2s = w2.at[pl.ds(0, width)], w2.at[pl.ds(HALF, width)]
        else:
            width = w2o_in.shape[1]
            w2o, w2s = w2.at[:, pl.ds(0, width)], w2.at[:, pl.ds(HALF, width)]
        pairs = (
            (w1_in, w1),
            (w2o_in, w2o),
            (w2s_in, w2s),
            (goal_o_in.at[at_out, lanes], goal.at[:, pl.ds(0, HALF)]),
            (goal_s_in.at[at_out, lanes], goal.at[:, pl.ds(HALF, HALF)]),
        )
        group = [
            pltpu.make_async_copy(src, dst, in_sem.at[5 * t + i])
            for i, (src, dst) in enumerate(pairs)
        ]
        for copy in group:
            copy.start()
        loads.append(group)
        if turned[t] and width < HALF:
            zeros = jnp.zeros((HALF - width, w2.shape[1]), bf16)
            w2[width:HALF] = zeros
            w2[HALF + width :] = zeros

    for copy in tokens:
        copy.wait()
    stores = []

    def send(t, i):
        copy_from = bufs[6 * t + 2 + i]
        target = outs[4 * t + i]
        target = target.at[:, at_out] if i == 3 else target.at[at_out]
        copy = pltpu.make_async_copy(copy_from, target, out_sem.at[4 * t + i])
        copy.start()
        stores.append(copy)

    for t in range(teachers):
        w1, w2, goal, hidden, pred, sums = bufs[6 * t : 6 * t + 6]
        channels = w1.shape[1]
        loads[t][0].wait()
        for m in range(0, rows, part):
            for n in range(0, channels, 512):
                to = min(n + 512, channels)
                hidden[m : m + part, n:to] = gelu(
                    jnp.dot(x[m : m + part], w1[:, n:to], preferred_element_type=f32)
                ).astype(bf16)
        send(t, 1)
        for copy in loads[t][1:]:
            copy.wait()
        send(t, 0)
        for m in range(0, rows, part):
            at = slice(m, m + part)
            p = lax.dot_general(
                hidden[at],
                w2[...],
                (((1,), (1 if turned[t] else 0,)), ((), ())),
                preferred_element_type=f32,
            )
            pred[at] = p
            wide = goal[at].astype(f32)
            pred_sq = jnp.sum(p * p, axis=1, keepdims=True)
            goal_sq = jnp.sum(wide * wide, axis=1, keepdims=True)
            cross = jnp.sum(p * wide, axis=1, keepdims=True)
            lane = lax.broadcasted_iota(jnp.int32, (part, 128), 1)
            cols = jnp.where(lane == 0, pred_sq, jnp.where(lane == 1, goal_sq, cross))
            sums[:, at] = jnp.transpose(cols)[:8]
        send(t, 2)
        send(t, 3)
    for copy in stores:
        copy.wait()


def adapt(pieces, which, goals, teachers, slots, prior=None):
    rows, width = sum(p.shape[0] for p in pieces), pieces[0].shape[1]
    turned = tuple(w2o.shape[0] != w1.shape[1] for w1, w2o, *_ in teachers)
    outs, scratch = [], [pltpu.VMEM((rows, width), bf16)]
    for (w1, *_), turn in zip(teachers, turned):
        channels = w1.shape[1]
        wide = 2 * HALF
        outs += [
            jax.ShapeDtypeStruct((2 * rows, wide), bf16),
            jax.ShapeDtypeStruct((2 * rows, channels), bf16),
            jax.ShapeDtypeStruct((2 * rows, wide), f32),
            jax.ShapeDtypeStruct((8, 2 * rows), f32),
        ]
        scratch += [
            pltpu.VMEM(w1.shape, bf16),
            pltpu.VMEM((wide, channels) if turn else (channels, wide), bf16),
            pltpu.VMEM((rows, wide), bf16),
            pltpu.VMEM((rows, channels), bf16),
            pltpu.VMEM((rows, wide), f32),
            pltpu.VMEM((8, rows), f32),
        ]
    n = len(teachers)
    held = sum(math.prod(b.shape) * jnp.dtype(b.dtype).itemsize for b in scratch)
    scratch += [
        pltpu.SemaphoreType.DMA((5 * n + len(pieces),)),
        pltpu.SemaphoreType.DMA((4 * n,)),
    ]
    args = [*pieces, *goals] + [a for teacher in teachers for a in teacher]
    aliases = {}
    if prior is not None:
        aliases = {len(args) + i: i for i in range(len(outs))}
        args += list(prior)
    anywhere = pl.BlockSpec(memory_space=pl.ANY)
    return pl.pallas_call(
        functools.partial(adapt_kernel, which, prior is None, turned, slots, len(pieces)),
        in_specs=[anywhere] * len(args),
        out_specs=[anywhere] * len(outs),
        out_shape=outs,
        scratch_shapes=scratch,
        input_output_aliases=aliases,
        compiler_params=pltpu.CompilerParams(vmem_limit_bytes=held + 3 * MIB),
        cost_estimate=pl.CostEstimate(flops=1000, bytes_accessed=1000, transcendentals=0),
        name="adapt",
    )(*args)


def shards(
    student,
    dino_feat,
    siglip_feat,
    sam_feat,
    w1_dino,
    w2_dino,
    w1_siglip,
    w2_siglip,
    w1_sam,
    w2_sam,
):
    n_images, row_count, grid, width = student.shape
    n_dp = lax.axis_size("dp")
    g = lax.axis_index("grp")
    total = n_images * n_dp * grid * grid
    own_tokens = n_images * row_count * grid

    own = student.reshape(own_tokens, width)
    cut = own_tokens * 3 // 8
    theirs = [lax.ppermute(piece, "grp", CHIP) for piece in (own[:cut], own[cut:])]

    w2s = (w2_dino, jnp.swapaxes(w2_sam, 0, 1), jnp.swapaxes(w2_siglip, 0, 1))
    w2_others = [lax.ppermute(w, "grp", CORE) for w in w2s]

    order = jnp.stack([g ^ 1, g ^ 3, g, g ^ 2]).astype(jnp.int32)
    kept, sent = targets(order, dino_feat, siglip_feat, sam_feat)
    sent, theirs[0], *w2_others = lax.optimization_barrier((sent, theirs[0], *w2_others))
    goals = (kept, lax.ppermute(sent, "grp", CORE))

    teachers = list(zip((w1_dino, w1_sam, w1_siglip), w2s, w2_others))
    firsts = adapt([own], 0, goals, teachers, (0, 1, 2))

    def second(i, after):
        pieces = list(theirs)
        if after is not None:
            *pieces, after = lax.optimization_barrier((*pieces, after))
        return adapt(pieces, 1, goals, teachers[i : i + 1], (i,), firsts[4 * i : 4 * i + 4])

    def gradient(state, after):
        goal, hidden, pred, part = state
        channels = hidden.shape[1]
        scale = channels / math.sqrt(total)
        sums = part + jnp.roll(lax.ppermute(part, "grp", CHIP), own_tokens, axis=1)
        pred_norm = jnp.sqrt(sums[0] + epsilon)
        goal_norm = jnp.sqrt(sums[1] + epsilon)
        product = pred_norm * goal_norm
        on_goal = -scale / product
        on_pred = scale * sums[2] / (product * pred_norm * pred_norm)
        on_goal, on_pred, after = lax.optimization_barrier((on_goal, on_pred, after))
        error = (on_goal[:, None] * goal.astype(f32) + on_pred[:, None] * pred).astype(bf16)
        return jnp.einsum("tk,tc->kc", hidden, error, preferred_element_type=f32)

    def between_cores(grad):
        sent_grad = lax.ppermute(grad[:, HALF:].astype(bf16), "grp", CORE)
        both = (grad[:, :HALF] + sent_grad.astype(f32)).astype(bf16)
        return both.reshape(n_dp, both.shape[0] // n_dp, HALF)

    def over_images(parts):
        split = lax.all_to_all(parts, "dp", 0, 0, tiled=True)
        return jnp.sum(split.astype(f32), axis=0)

    dino_state = second(0, None)
    sam_state = second(1, dino_state[3])
    dino_grad = gradient(dino_state, sam_state[3])
    siglip_state = second(2, dino_grad)
    dino_local = between_cores(dino_grad)
    sam_grad = gradient(sam_state, (dino_local, siglip_state[3]))
    siglip_grad = gradient(siglip_state, sam_grad)
    dino = over_images(dino_local)

    sam_local, siglip_local = between_cores(sam_grad), between_cores(siglip_grad)
    sam_width, siglip_width = w2_sam.shape[1], w2_siglip.shape[1]
    sam_rows, siglip_rows = sam_local.shape[1], siglip_local.shape[1]
    siglip_local = jnp.pad(siglip_local, ((0, 0), (0, sam_rows - siglip_rows), (0, 0)))
    rest = over_images(
        jnp.concatenate(
            [
                sam_local[..., :256],
                siglip_local[..., :256],
                sam_local[..., 256:sam_width],
                siglip_local[..., 256:siglip_width],
            ],
            axis=2,
        )
    )
    sam = jnp.concatenate([rest[:, :256], rest[:, 512 : 256 + sam_width]], axis=1)
    siglip = jnp.concatenate([rest[:, 256:512], rest[:, 256 + sam_width :]], axis=1)
    return dino, siglip[:siglip_rows], sam


def solution(mesh):
    in_specs = (
        P("dp", "grp", None, None),
        P("dp", None, None, "grp"),
        P("dp", None, None, "grp"),
        P("dp", None, None, "grp"),
        P(),
        P(None, "grp"),
        P(),
        P(None, "grp"),
        P(),
        P(None, "grp"),
    )
    out_specs = (P("dp", "grp"), P("dp", "grp"), P("dp", "grp"))
    return jax.shard_map(shards, mesh=mesh, in_specs=in_specs, out_specs=out_specs, check_vma=False)
```

profile of v0, /device:TPU:0, one launch (start us, length us, event | category | flops | bytes accessed | tf_op | source)
XLA Modules:
  0.0 146.1 jit_solution(14494250005682902906)
XLA Ops:
  1.3 1.9 %slice.133 = bf16[192,1280]{1,0:T(8,128)(2,1)} slice(bf16[512,1280]{1,0:T(8,128)(2,1)} %bitcast.27), slice={[0:192], [0:1280]} | slice | bytes 983040 | tf_op jit(solution)/shard_map/slice | solution.py:280
  4.8 2.0 %copy.27.dino = bf16[2,36,36,384]{3,2,1,0:T(8,128)(2,1)S(1)} copy(bf16[2,36,36,384]{3,0,2,1:T(2,128)(2,1)} %param.11) | data formatting | bytes 3981312 | tf_op args[1]
  8.4 3.6 %targets.1 = (bf16[2,2,256,1152]{3,2,1,0:T(8,128)(2,1)S(1)}, bf16[2,2,256,1152]{3,2,1,0:T(8,128)(2,1)S(1)}) custom-call(s32[4]{0:T(128)S(1)} %pad_add_fusion.order_ref, bf16[2,36,36,384]{3,2,1,0:T(8,128)(2,1)S(1)} %copy.27.dino, bf16[2,36,36,288]{3,2,1,0:T(8,128)(2,1)S(1)} %copy.28.siglip, bf16[2,32,32,320]{3,2,1,0:T(8,128)(2,1)S(1)} %copy-done.18), custom_call_target="tpu_custom_call" | custom-call | flops 1000 | bytes 1000 | tf_op jit(solution)/shard_map/targets/pallas_call | solution.py:87
  12.0 5.0 %collective-permute-done.refs_0_ = bf16[192,1280]{1,0:T(8,128)(2,1)S(1)} collective-permute-done((bf16[192,1280]{1,0:T(8,128)(2,1)}, bf16[192,1280]{1,0:T(8,128)(2,1)S(1)}, u32[]{:S(2)}, u32[]{:S(2)}) %collective-permute-start) | collective-permute-done | bytes 491552 | tf_op jit(solution)/shard_map/ppermute | solution.py:280
  17.1 1.9 %collective-permute-start.4 = (bf16[320,1280]{1,0:T(8,128)(2,1)S(1)}, bf16[320,1280]{1,0:T(8,128)(2,1)S(1)}, u32[]{:S(2)}, u32[]{:S(2)}) collective-permute-start(bf16[320,1280]{1,0:T(8,128)(2,1)S(1)} %slice.134), channel_id=1, source_target_pairs={{0,64},{32,96},{64,0},{96,32},{1,65},{33,97},{65,1},{97,33},{2,66}... | collective-permute-start | bytes 2457608 | tf_op jit(solution)/shard_map/ppermute | solution.py:280
  19.0 2.5 %collective-permute-done.5.refs_2_.refs_3_ = bf16[1024,1152]{1,0:T(8,128)(2,1)S(1)} collective-permute-done((bf16[1024,1152]{1,0:T(8,128)(2,1)S(1)}, bf16[1024,1152]{1,0:T(8,128)(2,1)S(1)}, u32[]{:S(2)}, u32[]{:S(2)}) %collective-permute-start.5) | collective-permute-done | bytes 2359328 | tf_op jit(solution)/shard_map/ppermute | solution.py:288
  22.8 15.4 %adapt.4 = (bf16[1024,768]{1,0:T(8,128)(2,1)S(1)}, bf16[1024,1536]{1,0:T(8,128)(2,1)}, f32[1024,768]{1,0:T(8,128)}, f32[8,1024]{1,0:T(8,128)S(1)}, bf16[1024,768...) custom-call(bf16[512,1280]{1,0:T(8,128)(2,1)S(1)} %bitcast.29, ...), custom_call_target="tpu_custom_call" | custom-call | flops 1000 | bytes 1000 | tf_op jit(solution)/shard_map/adapt/pallas_call | solution.py:247
  39.3 1.9 %copy-done.10 = bf16[1024,1536]{1,0:T(8,128)(2,1)S(1)} copy-done((bf16[1024,1536]{1,0:T(8,128)(2,1)S(1)}, bf16[1024,1536]{1,0:T(8,128)(2,1)}, u32[]{:S(2)}) %copy-start.10) | copy-done | bytes 3145752
  41.2 1.9 %copy-done.13 = f32[1024,768]{1,0:T(8,128)S(1)} copy-done((f32[1024,768]{1,0:T(8,128)S(1)}, f32[1024,768]{1,0:T(8,128)}, u32[]{:S(2)}) %copy-start.13) | copy-done | bytes 3145752
  44.5 5.5 %adapt.5 = (bf16[1024,768]{1,0:T(8,128)(2,1)S(1)}, bf16[1024,1536]{1,0:T(8,128)(2,1)S(1)}, f32[1024,768]{1,0:T(8,128)S(1)}, f32[8,1024]{1,0:T(8,128)S(1)}) custom-call(bf16[192,1280]{1,0:T(8,128)(2,1)S(1)} %collective-permute-done.refs_0_, ...), custom_call_target="tpu_custom_call", output_to_operand_aliasing={{0}: (7, {}), {1}: (8, {}), {2}: (9, {}), {3}: (10, {})} | custom-call | flops 1000 | bytes 1000 | tf_op jit(solution)/shard_map/adapt/pallas_call | solution.py:247
  53.4 4.9 %adapt.6 = (bf16[1024,768]{1,0:T(8,128)(2,1)S(1)}, bf16[1024,1280]{1,0:T(8,128)(2,1)S(1)}, f32[1024,768]{1,0:T(8,128)S(1)}, f32[8,1024]{1,0:T(8,128)S(1)}) custom-call(bf16[192,1280]{1,0:T(8,128)(2,1)S(1)} %collective-permute-done.refs_0_, ...), custom_call_target="tpu_custom_call", output_to_operand_aliasing={{0}: (7, {}), {1}: (8, {}), {2}: (9, {}), {3}: (10, {})} | custom-call | flops 1000 | bytes 1000 | tf_op jit(solution)/shard_map/adapt/pallas_call | solution.py:247
  58.8 6.4 %fusion.3 = f32[1536,768]{1,0:T(8,128)} fusion(bf16[1024,1536]{1,0:T(8,128)(2,1)S(1)} %copy-done.12, f32[1024,768]{1,0:T(8,128)S(1)} %get-tuple-element.67, bf16[1024,768]{1,0:T(8,128)(2,1)} %copy-done.17, f32[1024]{0:T(1024)S(1)} %get-tuple-element.66, f32[1024]{0:T(1024)S(1)} %get-tuple-element.64), kind=kOutput, calls=%fused_computation.15 | convolution fusion | flops 2419851264 | bytes 12591104 | tf_op jit(solution)/shard_map/tk,tc->kc/dot_general | solution.py:311
  65.3 1.9 %slice.197 = bf16[1536,384]{1,0:T(8,128)(2,1)S(1)} slice(f32[1536,768]{1,0:T(8,128)} %fusion.3), slice={[0:1536], [384:768]} | slice | bytes 2359296 | tf_op jit(solution)/shard_map/slice | solution.py:314
  67.4 5.1 %adapt.7 = (bf16[1024,768]{1,0:T(8,128)(2,1)S(1)}, bf16[1024,1152]{1,0:T(8,128)(2,1)S(1)}, f32[1024,768]{1,0:T(8,128)S(1)}, f32[8,1024]{1,0:T(8,128)S(1)}) custom-call(bf16[192,1280]{1,0:T(8,128)(2,1)S(1)} %collective-permute-done.refs_0_, ...), custom_call_target="tpu_custom_call", output_to_operand_aliasing={{0}: (7, {}), {1}: (8, {}), {2}: (9, {}), {3}: (10, {})} | custom-call | flops 1000 | bytes 1000 | tf_op jit(solution)/shard_map/adapt/pallas_call | solution.py:247
  72.5 2.0 %collective-permute-start.10 = (f32[8,1024]{1,0:T(8,128)S(1)}, f32[8,1024]{1,0:T(8,128)S(1)}, u32[]{:S(2)}, u32[]{:S(2)}) collective-permute-start(f32[8,1024]{1,0:T(8,128)S(1)} %get-tuple-element.75), channel_id=1, source_target_pairs={{0,64},{32,96},{64,0},{96,32},{1,65},{33,97},{65,1},{97,33},{2,66}... | collective-permute-start | bytes 98312 | tf_op jit(solution)/shard_map/ppermute | solution.py:303
  74.5 2.2 %collective-permute-done.10 = f32[8,1024]{1,0:T(8,128)S(1)} collective-permute-done((f32[8,1024]{1,0:T(8,128)S(1)}, f32[8,1024]{1,0:T(8,128)S(1)}, u32[]{:S(2)}, u32[]{:S(2)}) %collective-permute-start.10) | collective-permute-done | bytes 32800 | tf_op jit(solution)/shard_map/ppermute | solution.py:303
  78.3 2.5 %fusion.4 = f32[1280,768]{1,0:T(8,128)S(1)} fusion(bf16[1024,1280]{1,0:T(8,128)(2,1)S(1)} %get-tuple-element.68, f32[1024,768]{1,0:T(8,128)S(1)} %get-tuple-element.79, bf16[1024,768]{1,0:T(8,128)(2,1)S(1)} %get-tuple-element.77, f32[1024]{0:T(1024)S(1)} %get-tuple-element.78, f32[1024]{0:T(1024)S(1)} %get-tuple-element.76), kind=kOutput, calls=%fused_computation.16 | convolution fusion | flops 2017198080 | bytes 11280384 | tf_op jit(solution)/shard_map/tk,tc->kc/dot_general | solution.py:311
  80.9 2.3 %fusion.5 = f32[1152,768]{1,0:T(8,128)S(1)} fusion(bf16[1024,1152]{1,0:T(8,128)(2,1)S(1)} %get-tuple-element.80, f32[1024,768]{1,0:T(8,128)S(1)} %get-tuple-element.84, bf16[1024,768]{1,0:T(8,128)(2,1)S(1)} %get-tuple-element.82, f32[1024]{0:T(1024)S(1)} %get-tuple-element.83, f32[1024]{0:T(1024)S(1)} %get-tuple-element.81), kind=kOutput, calls=%fused_computation.17 | convolution fusion | flops 1815871488 | bytes 10625024 | tf_op jit(solution)/shard_map/tk,tc->kc/dot_general | solution.py:311
  85.9 10.9 %all-to-all-start = ((bf16[32,48,384]{2,1,0:T(8,128)(2,1)}), bf16[32,48,384]{2,1,0:T(8,128)(2,1)S(1)}, u32[]{:S(2)}, u32[]{:S(2)}) async-start(bf16[32,48,384]{2,1,0:T(8,128)(2,1)} %bitcast.12), calls=%async_computation | async-start | bytes 2359296 | tf_op jit(solution)/shard_map/all_to_all | solution.py:319
  96.8 2.6 %fusion.2 = bf16[1152,384]{1,0:T(8,128)(2,1)} fusion(f32[1152,768]{1,0:T(8,128)} %copy-done.20, bf16[1152,384]{1,0:T(8,128)(2,1)S(1)} %collective-permute-done.11), kind=kLoop, calls=%fused_computation.13 | loop fusion | flops 1327104 | bytes 3538944 | tf_op jit(solution)/shard_map/convert_element_type | solution.py:315
  100.8 2.0 %fusion.1 = bf16[1280,384]{1,0:T(8,128)(2,1)S(1)} fusion(f32[1280,768]{1,0:T(8,128)} %copy-done.19, bf16[1280,384]{1,0:T(8,128)(2,1)} %collective-permute-done.9), kind=kLoop, calls=%fused_computation.10 | loop fusion | flops 1474560 | bytes 3932160 | tf_op jit(solution)/shard_map/convert_element_type | solution.py:315
  104.3 11.7 %all-to-all-done = bf16[32,48,384]{2,1,0:T(8,128)(2,1)S(1)} async-done(((bf16[32,48,384]{2,1,0:T(8,128)(2,1)}), bf16[32,48,384]{2,1,0:T(8,128)(2,1)S(1)}, u32[]{:S(2)}, u32[]{:S(2)}) %all-to-all-start) | async-done | bytes 1179680 | tf_op jit(solution)/shard_map/all_to_all | solution.py:319
  116.0 5.3 %all-to-all-start.1 = ((bf16[32,40,608]{2,1,0:T(8,128)(2,1)}), bf16[32,40,608]{2,1,0:T(8,128)(2,1)S(1)}, u32[]{:S(2)}, u32[]{:S(2)}) async-start(bf16[32,40,608]{2,1,0:T(8,128)(2,1)} %pad_maximum_fusion), calls=%async_computation.1 | async-start | bytes 3276800 | tf_op jit(solution)/shard_map/all_to_all | solution.py:319
  122.1 22.3 %all-to-all-done.1 = bf16[32,40,608]{2,1,0:T(8,128)(2,1)S(1)} async-done(((bf16[32,40,608]{2,1,0:T(8,128)(2,1)}), bf16[32,40,608]{2,1,0:T(8,128)(2,1)S(1)}, u32[]{:S(2)}, u32[]{:S(2)}) %all-to-all-start.1) | async-done | bytes 1556512 | tf_op jit(solution)/shard_map/all_to_all | solution.py:319
  (97 shorter events, 21.2 us)
Async XLA Ops:
  0.6 16.3 %collective-permute-start.1 = (bf16[1536,384]{1,0:T(8,128)(2,1)}, bf16[1536,384]{1,0:T(8,128)(2,1)S(1)}, u32[]{:S(2)}, u32[]{:S(2)}) collective-permute-start(bf16[1536,384]{1,0:T(8,128)(2,1)} %refs_5_.1), channel_id=1, source_target_pairs={{0,32},{32,0},{64,96},{96,64},{1,33},{33,1},{65,97},{97,65},{2,34}... | collective-permute-start | bytes 3538952 | tf_op jit(solution)/shard_map/ppermute | solution.py:283
  0.7 16.2 %collective-permute-start.2 = (bf16[320,1280]{1,0:T(8,128)(2,1)}, bf16[320,1280]{1,0:T(8,128)(2,1)S(1)}, u32[]{:S(2)}, u32[]{:S(2)}) collective-permute-start(bf16[320,1280]{1,0:T(8,128)(2,1)} %bitcast.30), channel_id=1, source_target_pairs={{0,32},{32,0},{64,96},{96,64},{1,33},{33,1},{65,97},{97,65},{2,34}... | collective-permute-start | bytes 2457608 | tf_op jit(solution)/shard_map/ppermute | solution.py:283
  1.2 15.7 %collective-permute-start.3 = (bf16[288,1152]{1,0:T(8,128)(2,1)}, bf16[288,1152]{1,0:T(8,128)(2,1)S(1)}, u32[]{:S(2)}, u32[]{:S(2)}) collective-permute-start(bf16[288,1152]{1,0:T(8,128)(2,1)} %bitcast.33), channel_id=1, source_target_pairs={{0,32},{32,0},{64,96},{96,64},{1,33},{33,1},{65,97},{97,65},{2,34}... | collective-permute-start | bytes 1990664 | tf_op jit(solution)/shard_map/ppermute | solution.py:283
  3.2 13.8 %collective-permute-start = (bf16[192,1280]{1,0:T(8,128)(2,1)}, bf16[192,1280]{1,0:T(8,128)(2,1)S(1)}, u32[]{:S(2)}, u32[]{:S(2)}) collective-permute-start(bf16[192,1280]{1,0:T(8,128)(2,1)} %slice.133), channel_id=1, source_target_pairs={{0,64},{32,96},{64,0},{96,32},{1,65},{33,97},{65,1},{97,33},{2,66}... | collective-permute-start | bytes 1474568 | tf_op jit(solution)/shard_map/ppermute | solution.py:280
  8.4 8.7 %copy-start.3 = (bf16[2,8,32,1280]{3,2,1,0:T(8,128)(2,1)S(1)}, bf16[2,8,32,1280]{3,2,1,0:T(8,128)(2,1)}, u32[]{:S(2)}) copy-start(bf16[2,8,32,1280]{3,2,1,0:T(8,128)(2,1)} %param.10) | copy-start | bytes 3932164
  8.4 13.2 %copy-start.2 = (bf16[1280,1152]{1,0:T(8,128)(2,1)S(1)}, bf16[1280,1152]{1,0:T(8,128)(2,1)}, u32[]{:S(2)}) copy-start(bf16[1280,1152]{1,0:T(8,128)(2,1)} %refs_4_.7) | copy-start | bytes 8847364
  8.4 13.2 %copy-start.4 = (bf16[1536,384]{1,0:T(8,128)(2,1)S(1)}, bf16[1536,384]{1,0:T(8,128)(2,1)}, u32[]{:S(2)}) copy-start(bf16[1536,384]{1,0:T(8,128)(2,1)} %refs_5_.1) | copy-start | bytes 3538948
  8.4 13.2 %copy-start.5 = (bf16[1280,320]{0,1:T(8,128)(2,1)S(1)}, bf16[1280,320]{0,1:T(8,128)(2,1)}, u32[]{:S(2)}) copy-start(bf16[1280,320]{0,1:T(8,128)(2,1)} %param.19) | copy-start | bytes 2457604
  8.4 13.2 %copy-start.14 = (bf16[1152,288]{0,1:T(8,128)(2,1)S(1)}, bf16[1152,288]{0,1:T(8,128)(2,1)}, u32[]{:S(2)}) copy-start(bf16[1152,288]{0,1:T(8,128)(2,1)} %param.17) | copy-start | bytes 1990660
  17.0 4.6 %collective-permute-start.5 = (bf16[1024,1152]{1,0:T(8,128)(2,1)S(1)}, bf16[1024,1152]{1,0:T(8,128)(2,1)S(1)}, u32[]{:S(2)}, u32[]{:S(2)}) collective-permute-start(bf16[1024,1152]{1,0:T(8,128)(2,1)S(1)} %bitcast.36), channel_id=1, source_target_pairs={{0,32},{32,0},{64,96},{96,64},{1,33},{33,1},{65,97},{97,65},{2,34}... | collective-permute-start | bytes 7077896 | tf_op jit(solution)/shard_map/ppermute | solution.py:288
  17.1 21.0 %collective-permute-start.4 = (bf16[320,1280]{1,0:T(8,128)(2,1)S(1)}, bf16[320,1280]{1,0:T(8,128)(2,1)S(1)}, u32[]{:S(2)}, u32[]{:S(2)}) collective-permute-start(bf16[320,1280]{1,0:T(8,128)(2,1)S(1)} %slice.134), channel_id=1, source_target_pairs={{0,64},{32,96},{64,0},{96,32},{1,65},{33,97},{65,1},{97,33},{2,66}... | collective-permute-start | bytes 2457608 | tf_op jit(solution)/shard_map/ppermute | solution.py:280
  22.8 16.6 %copy-start = (bf16[1280,1536]{1,0:T(8,128)(2,1)S(1)}, bf16[1280,1536]{1,0:T(8,128)(2,1)}, u32[]{:S(2)}) copy-start(bf16[1280,1536]{1,0:T(8,128)(2,1)} %refs_4_.5) | copy-start | bytes 11796484
  44.5 8.9 %copy-start.1 = (bf16[1280,1280]{1,0:T(8,128)(2,1)S(1)}, bf16[1280,1280]{1,0:T(8,128)(2,1)}, u32[]{:S(2)}) copy-start(bf16[1280,1280]{1,0:T(8,128)(2,1)} %refs_4_.6) | copy-start | bytes 9830404
  44.5 8.9 %copy-start.9 = (f32[1024,768]{1,0:T(8,128)S(1)}, f32[1024,768]{1,0:T(8,128)}, u32[]{:S(2)}) copy-start(f32[1024,768]{1,0:T(8,128)} %get-tuple-element.61.refs_9_) | copy-start | bytes 9437188
  51.8 7.0 %collective-permute-start.6 = (f32[8,1024]{1,0:T(8,128)S(1)}, f32[8,1024]{1,0:T(8,128)S(1)}, u32[]{:S(2)}, u32[]{:S(2)}) collective-permute-start(f32[8,1024]{1,0:T(8,128)S(1)} %get-tuple-element.56), channel_id=1, source_target_pairs={{0,64},{32,96},{64,0},{96,32},{1,65},{33,97},{65,1},{97,33},{2,66}... | collective-permute-start | bytes 98312 | tf_op jit(solution)/shard_map/ppermute | solution.py:303
  58.3 9.0 %collective-permute-start.8 = (f32[8,1024]{1,0:T(8,128)S(1)}, f32[8,1024]{1,0:T(8,128)S(1)}, u32[]{:S(2)}, u32[]{:S(2)}) collective-permute-start(f32[8,1024]{1,0:T(8,128)S(1)} %get-tuple-element.63), channel_id=1, source_target_pairs={{0,64},{32,96},{64,0},{96,32},{1,65},{33,97},{65,1},{97,33},{2,66}... | collective-permute-start | bytes 98312 | tf_op jit(solution)/shard_map/ppermute | solution.py:303
  65.3 11.6 %slice-start = ((s8[4718592]{0:T(1024)(128)(4,1)}), s8[4194304]{0:T(1024)(128)(4,1)S(1)}, s32[]{:S(2)}) async-start(s8[4718592]{0:T(1024)(128)(4,1)} %bitcast.39), calls=%async_computation.2 | async-start | bytes 8388608
  67.2 9.6 %collective-permute-start.7 = (bf16[1536,384]{1,0:T(8,128)(2,1)S(1)}, bf16[1536,384]{1,0:T(8,128)(2,1)S(1)}, u32[]{:S(2)}, u32[]{:S(2)}) collective-permute-start(bf16[1536,384]{1,0:T(8,128)(2,1)S(1)} %slice.197), channel_id=1, source_target_pairs={{0,32},{32,0},{64,96},{96,64},{1,33},{33,1},{65,97},{97,65},{2,34}... | collective-permute-start | bytes 3538952 | tf_op jit(solution)/shard_map/ppermute | solution.py:314
  67.4 9.5 %slice-start.1 = ((s8[4718592]{0:T(1024)(128)(4,1)}), s8[524288]{0:T(1024)(128)(4,1)S(1)}, s32[]{:S(2)}) async-start(s8[4718592]{0:T(1024)(128)(4,1)} %bitcast.39), calls=%async_computation.3 | async-start | bytes 1048576
  72.5 4.3 %collective-permute-start.10 = (f32[8,1024]{1,0:T(8,128)S(1)}, f32[8,1024]{1,0:T(8,128)S(1)}, u32[]{:S(2)}, u32[]{:S(2)}) collective-permute-start(f32[8,1024]{1,0:T(8,128)S(1)} %get-tuple-element.75), channel_id=1, source_target_pairs={{0,64},{32,96},{64,0},{96,32},{1,65},{33,97},{65,1},{97,33},{2,66}... | collective-permute-start | bytes 98312 | tf_op jit(solution)/shard_map/ppermute | solution.py:303
  84.3 12.5 %collective-permute-start.11 = (bf16[1152,384]{1,0:T(8,128)(2,1)}, bf16[1152,384]{1,0:T(8,128)(2,1)S(1)}, u32[]{:S(2)}, u32[]{:S(2)}) collective-permute-start(bf16[1152,384]{1,0:T(8,128)(2,1)} %slice.199), channel_id=1, source_target_pairs={{0,32},{32,0},{64,96},{96,64},{1,33},{33,1},{65,97},{97,65},{2,34}... | collective-permute-start | bytes 2654216 | tf_op jit(solution)/shard_map/ppermute | solution.py:314
  85.6 15.1 %collective-permute-start.9 = (bf16[1280,384]{1,0:T(8,128)(2,1)}, bf16[1280,384]{1,0:T(8,128)(2,1)}, u32[]{:S(2)}, u32[]{:S(2)}) collective-permute-start(bf16[1280,384]{1,0:T(8,128)(2,1)} %slice.198), channel_id=1, source_target_pairs={{0,32},{32,0},{64,96},{96,64},{1,33},{33,1},{65,97},{97,65},{2,34}... | collective-permute-start | bytes 2949128 | tf_op jit(solution)/shard_map/ppermute | solution.py:314
  85.9 30.1 %all-to-all-start = ((bf16[32,48,384]{2,1,0:T(8,128)(2,1)}), bf16[32,48,384]{2,1,0:T(8,128)(2,1)S(1)}, u32[]{:S(2)}, u32[]{:S(2)}) async-start(bf16[32,48,384]{2,1,0:T(8,128)(2,1)} %bitcast.12), calls=%async_computation | async-start | bytes 2359296 | tf_op jit(solution)/shard_map/all_to_all | solution.py:319
  116.0 28.4 %all-to-all-start.1 = ((bf16[32,40,608]{2,1,0:T(8,128)(2,1)}), bf16[32,40,608]{2,1,0:T(8,128)(2,1)S(1)}, u32[]{:S(2)}, u32[]{:S(2)}) async-start(bf16[32,40,608]{2,1,0:T(8,128)(2,1)} %pad_maximum_fusion), calls=%async_computation.1 | async-start | bytes 3276800 | tf_op jit(solution)/shard_map/all_to_all | solution.py:319
  (14 other events, 43.7 us)
where the time goes:
time: 147 us; the launch traced here: 146 us
  waiting for transfers between devices  43.8 us (30%)
  Pallas kernels  34.4 us (23%)
  starting transfers between devices  25 us (17%)
  local copies, waits for them, and re-layouts  20.5 us (14%)
  matrix products  11.3 us (8%)
  other arithmetic  9.98 us (7%)
    all_to_all x2, waiting for transfers between devices, over_images(): split = lax.all_to_all(parts, 'dp', 0, 0, tiled=True)  34.1 us
    pallas_call x4, Pallas kernels, adapt(): pl.pallas_call(functools.partial(adapt_kernel, which, prior is None, turn...  30.9 us
    all_to_all x2, starting transfers between devices, over_images(): split = lax.all_to_all(parts, 'dp', 0, 0, tiled=True)  16.2 us
    unnamed x50, local copies, waits for them, and re-layouts  12.7 us
    dot_general x3, matrix products, gradient(): return jnp.einsum('tk,tc->kc', hidden, error, preferred_element_type=f32)  11.3 us
    convert_element_type x3, other arithmetic, between_cores(): both = (grad[:, :HALF] + sent_grad.astype(f32)).astype(bf16)  6.03 us
    ppermute x2, waiting for transfers between devices, shards(): lax.ppermute(piece, 'grp', CHIP)  4.96 us
    slice x3, local copies, waits for them, and re-layouts, between_cores(): sent_grad = lax.ppermute(grad[:, HALF:].astype(bf16), 'grp', CORE)  4.32 us
  transfers between devices with their start and end apart: 14, of which 5 were waited for; matrix products, arithmetic and copies ran while one was open for 15% of the time, Pallas kernels for 20%

commit v1 on v0

--- a/solution.py
+++ b/solution.py
@@ -106,6 +106,10 @@
     return half + half * jnp.tanh(inner)
 
 
+def column_runs(channels):
+    return [(n, min(n + 512, channels)) for n in range(0, channels, 512)]
+
+
 def copies_of(refs, n):
     return refs[:n], refs[n:]
 
@@ -120,7 +124,7 @@
     outs, refs = copies_of(refs, 4 * teachers)
     x, refs = refs[0], refs[1:]
     bufs, refs = copies_of(refs, 6 * teachers)
-    in_sem, out_sem = refs
+    in_sem, w1_sem, out_sem = refs
     rows = x.shape[0]
     part = 256
     at_out = pl.ds(which * rows, rows)
@@ -144,8 +148,15 @@
         else:
             width = w2o_in.shape[1]
             w2o, w2s = w2.at[:, pl.ds(0, width)], w2.at[:, pl.ds(HALF, width)]
+        strips = [
+            pltpu.make_async_copy(
+                w1_in.at[:, pl.ds(n, to - n)],
+                w1.at[:, pl.ds(n, to - n)],
+                w1_sem.at[4 * t + i],
+            )
+            for i, (n, to) in enumerate(column_runs(w1.shape[1]))
+        ]
         pairs = (
-            (w1_in, w1),
             (w2o_in, w2o),
             (w2s_in, w2s),
             (goal_o_in.at[at_out, lanes], goal.at[:, pl.ds(0, HALF)]),
@@ -155,9 +166,9 @@
             pltpu.make_async_copy(src, dst, in_sem.at[5 * t + i])
             for i, (src, dst) in enumerate(pairs)
         ]
-        for copy in group:
+        for copy in strips + group:
             copy.start()
-        loads.append(group)
+        loads.append((strips, group))
         if turned[t] and width < HALF:
             zeros = jnp.zeros((HALF - width, w2.shape[1]), bf16)
             w2[width:HALF] = zeros
@@ -178,15 +189,15 @@
     for t in range(teachers):
         w1, w2, goal, hidden, pred, sums = bufs[6 * t : 6 * t + 6]
         channels = w1.shape[1]
-        loads[t][0].wait()
-        for m in range(0, rows, part):
-            for n in range(0, channels, 512):
-                to = min(n + 512, channels)
+        strips, group = loads[t]
+        for strip, (n, to) in zip(strips, column_runs(channels)):
+            strip.wait()
+            for m in range(0, rows, part):
                 hidden[m : m + part, n:to] = gelu(
                     jnp.dot(x[m : m + part], w1[:, n:to], preferred_element_type=f32)
                 ).astype(bf16)
         send(t, 1)
-        for copy in loads[t][1:]:
+        for copy in group:
             copy.wait()
         send(t, 0)
         for m in range(0, rows, part):
@@ -237,6 +248,7 @@
     scratch += [
         pltpu.SemaphoreType.DMA((5 * n + len(pieces),)),
         pltpu.SemaphoreType.DMA((4 * n,)),
+        pltpu.SemaphoreType.DMA((4 * n,)),
     ]
     args = [*pieces, *goals] + [a for teacher in teachers for a in teacher]
     aliases = {}
@@ -251,10 +263,60 @@
         out_shape=outs,
         scratch_shapes=scratch,
         input_output_aliases=aliases,
-        compiler_params=pltpu.CompilerParams(vmem_limit_bytes=held + 3 * MIB),
+        compiler_params=pltpu.CompilerParams(vmem_limit_bytes=max(held + 3 * MIB, 44 * MIB)),
         cost_estimate=pl.CostEstimate(flops=1000, bytes_accessed=1000, transcendentals=0),
         name="adapt",
     )(*args)
+
+
+def pack_kernel(blocks, dino, dino_other, sam, sam_other, siglip, siglip_other, out):
+    sums = [
+        a[...].astype(f32) + b[...].astype(f32)
+        for a, b in ((dino, dino_other), (sam, sam_other), (siglip, siglip_other))
+    ]
+    rows = [total.shape[0] // blocks for total in sums]
+    tall = rows[1]
+    for j in range(blocks):
+        d, m, s = [total[j * r : (j + 1) * r] for total, r in zip(sums, rows)]
+        s = jnp.concatenate([s, jnp.zeros((tall - rows[2], HALF), f32)], axis=0)
+        mixed = m[:, 256:] + pltpu.roll(s[:, 256:], 64, 1)
+        strips = [d[:, :128], d[:, 128:256], d[:, 256:], m[:, :128], m[:, 128:256], mixed]
+        strips += [s[:, :128], s[:, 128:256]]
+        count = sum(strip.shape[0] for strip in strips)
+        strips.append(jnp.zeros((out.shape[1] - count, 128), f32))
+        out[j] = jnp.concatenate(strips, axis=0).astype(bf16)
+
+
+def pack(grads, received, n_dp):
+    blocks = 4
+    steps = n_dp // blocks
+    rows = [g.shape[0] // n_dp for g in grads]
+    height = -(-(3 * rows[0] + 5 * rows[1]) // 16) * 16
+    args, specs = [], []
+    for grad, other, r in zip(grads, received, rows):
+        args += [grad, other]
+        specs += [pl.BlockSpec((r * blocks, HALF), lambda i: (i, 0))] * 2
+    return pl.pallas_call(
+        functools.partial(pack_kernel, blocks),
+        grid=(steps,),
+        in_specs=specs,
+        out_specs=pl.BlockSpec((blocks, height, 128), lambda i: (i, 0, 0)),
+        out_shape=jax.ShapeDtypeStruct((n_dp, height, 128), bf16),
+        compiler_params=pltpu.CompilerParams(vmem_limit_bytes=16 * MIB),
+        name="pack",
+    )(*args)
+
+
+def unpack(total, rows):
+    dino, sam, siglip = rows
+    at = 3 * dino
+    mixed = total[at + 2 * sam : at + 3 * sam]
+    low = at + 3 * sam
+    return (
+        jnp.concatenate([total[i * dino : (i + 1) * dino] for i in range(3)], axis=1),
+        jnp.concatenate([total[low : low + siglip], total[low + sam : low + sam + siglip], mixed[:siglip, 64:96]], axis=1),
+        jnp.concatenate([total[at : at + sam], total[at + sam : at + 2 * sam], mixed[:, :64]], axis=1),
+    )
 
 
 def shards(
@@ -276,7 +338,7 @@
     own_tokens = n_images * row_count * grid
 
     own = student.reshape(own_tokens, width)
-    cut = own_tokens * 3 // 8
+    cut = own_tokens // 4
     theirs = [lax.ppermute(piece, "grp", CHIP) for piece in (own[:cut], own[cut:])]
 
     w2s = (w2_dino, jnp.swapaxes(w2_sam, 0, 1), jnp.swapaxes(w2_siglip, 0, 1))
@@ -290,11 +352,12 @@
     teachers = list(zip((w1_dino, w1_sam, w1_siglip), w2s, w2_others))
     firsts = adapt([own], 0, goals, teachers, (0, 1, 2))
 
-    def second(i, after):
+    def second(i, to, after=None):
         pieces = list(theirs)
         if after is not None:
             *pieces, after = lax.optimization_barrier((*pieces, after))
-        return adapt(pieces, 1, goals, teachers[i : i + 1], (i,), firsts[4 * i : 4 * i + 4])
+        slots = tuple(range(i, to))
+        return adapt(pieces, 1, goals, teachers[i:to], slots, firsts[4 * i : 4 * to])
 
     def gradient(state, after):
         goal, hidden, pred, part = state
@@ -308,44 +371,20 @@
         on_pred = scale * sums[2] / (product * pred_norm * pred_norm)
         on_goal, on_pred, after = lax.optimization_barrier((on_goal, on_pred, after))
         error = (on_goal[:, None] * goal.astype(f32) + on_pred[:, None] * pred).astype(bf16)
-        return jnp.einsum("tk,tc->kc", hidden, error, preferred_element_type=f32)
-
-    def between_cores(grad):
-        sent_grad = lax.ppermute(grad[:, HALF:].astype(bf16), "grp", CORE)
-        both = (grad[:, :HALF] + sent_grad.astype(f32)).astype(bf16)
-        return both.reshape(n_dp, both.shape[0] // n_dp, HALF)
-
-    def over_images(parts):
-        split = lax.all_to_all(parts, "dp", 0, 0, tiled=True)
-        return jnp.sum(split.astype(f32), axis=0)
-
-    dino_state = second(0, None)
-    sam_state = second(1, dino_state[3])
-    dino_grad = gradient(dino_state, sam_state[3])
-    siglip_state = second(2, dino_grad)
-    dino_local = between_cores(dino_grad)
-    sam_grad = gradient(sam_state, (dino_local, siglip_state[3]))
-    siglip_grad = gradient(siglip_state, sam_grad)
-    dino = over_images(dino_local)
-
-    sam_local, siglip_local = between_cores(sam_grad), between_cores(siglip_grad)
-    sam_width, siglip_width = w2_sam.shape[1], w2_siglip.shape[1]
-    sam_rows, siglip_rows = sam_local.shape[1], siglip_local.shape[1]
-    siglip_local = jnp.pad(siglip_local, ((0, 0), (0, sam_rows - siglip_rows), (0, 0)))
-    rest = over_images(
-        jnp.concatenate(
-            [
-                sam_local[..., :256],
-                siglip_local[..., :256],
-                sam_local[..., 256:sam_width],
-                siglip_local[..., 256:siglip_width],
-            ],
-            axis=2,
-        )
+        grad = jnp.einsum("tk,tc->kc", hidden, error, preferred_element_type=f32)
+        return grad.astype(bf16)
+
+    dino_state = second(0, 1)
+    others = second(1, 3, dino_state[3])
+    sam_state, siglip_state = others[:4], others[4:]
+    grads = [gradient(dino_state, sam_state[3])]
+    grads.append(gradient(sam_state, grads[0]))
+    grads.append(gradient(siglip_state, grads[1]))
+    received = [lax.ppermute(grad[:, HALF:], "grp", CORE) for grad in grads]
+    split = lax.all_to_all(pack(grads, received, n_dp), "dp", 0, 0, tiled=True)
+    return unpack(
+        jnp.sum(split.astype(f32), axis=0), [w.shape[0] // n_dp for w in (w2_dino, w2_sam, w2_siglip)]
     )
-    sam = jnp.concatenate([rest[:, :256], rest[:, 512 : 256 + sam_width]], axis=1)
-    siglip = jnp.concatenate([rest[:, 256:512], rest[:, 256 + sam_width :]], axis=1)
-    return dino, siglip[:siglip_rows], sam
 
 
 def solution(mesh):

time: 147 us -> 127 us (0.86)
  blocking collectives: 0 us -> 48.5 us
  waiting for transfers between devices: 43.8 us -> 7.39 us
  starting transfers between devices: 25 us -> 8.89 us
  local copies, waits for them, and re-layouts: 20.5 us -> 11.6 us
  other arithmetic: 9.98 us -> 2.52 us
  Pallas kernels: 34.4 us -> 39.5 us
  matrix products: 11.3 us -> 7.71 us
    all_to_all x0 -> x1, blocking collectives: none -> 48.5 us  [shards(): split = lax.all_to_all(pack(grads, received, n_dp), 'dp', 0, 0, tiled=True)]
    all_to_all x2 -> x0, waiting for transfers between devices: 34.1 us -> none  [over_images(): split = lax.all_to_all(parts, 'dp', 0, 0, tiled=True)]
    all_to_all x2 -> x0, starting transfers between devices: 16.2 us -> none  [over_images(): split = lax.all_to_all(parts, 'dp', 0, 0, tiled=True)]
    convert_element_type x3 -> x0, other arithmetic: 6.03 us -> none  [between_cores(): both = (grad[:, :HALF] + sent_grad.astype(f32)).astype(bf16)]
    slice x10 -> x8, local copies, waits for them, and re-layouts: 4.62 us -> 0.4 us  [the longest x3 0.31 us: shards(): received = [lax.ppermute(grad[:, HALF:], 'grp', CORE) for grad in grads]]
    dot_general x3, matrix products: 11.3 us -> 7.71 us  [gradient(): grad = jnp.einsum('tk,tc->kc', hidden, error, preferred_element_type=f32)]
    pallas_call x4 -> x3, Pallas kernels: 30.9 us -> 34.3 us  [adapt(): pl.pallas_call(functools.partial(adapt_kernel, which, prior is None, turn...]
    ppermute x2, waiting for transfers between devices: 4.96 us -> 2.29 us  [shards(): lax.ppermute(piece, 'grp', CHIP)]
  transfers between devices with their start and end apart: 14 -> 12, of which waited for: 5 -> 3; matrix products, arithmetic and copies ran while one was open for 15% -> 9% of each run, Pallas kernels for 20% -> 24%
where the time goes in v1:
time: 127 us
  blocking collectives  48.5 us (38%)
  Pallas kernels  39.5 us (31%)
  local copies, waits for them, and re-layouts  11.6 us (9%)
  starting transfers between devices  8.89 us (7%)
  matrix products  7.71 us (6%)
  waiting for transfers between devices  7.39 us (6%)
  other arithmetic  2.52 us (2%)
    all_to_all x1, blocking collectives, shards(): split = lax.all_to_all(pack(grads, received, n_dp), 'dp', 0, 0, tiled=True)  48.5 us
    pallas_call x3, Pallas kernels, adapt(): pl.pallas_call(functools.partial(adapt_kernel, which, prior is None, turn...  34.3 us
    unnamed x44, local copies, waits for them, and re-layouts  10.1 us
    dot_general x3, matrix products, gradient(): grad = jnp.einsum('tk,tc->kc', hidden, error, preferred_element_type=f32)  7.71 us
    ppermute x3, starting transfers between devices, gradient(): sums = part + jnp.roll(lax.ppermute(part, 'grp', CHIP), own_tokens, axis=1)  3.69 us
    pallas_call x1, Pallas kernels, targets(): pl.pallas_call(targets_kernel, grid_spec=pltpu.PrefetchScalarGridSpec(num...  3.56 us
    ppermute x2, starting transfers between devices, shards(): lax.ppermute(piece, 'grp', CHIP)  3.36 us
    ppermute x1, waiting for transfers between devices, shards(): goals = (kept, lax.ppermute(sent, 'grp', CORE))  2.69 us
  transfers between devices with their start and end apart: 12, of which 3 were waited for; matrix products, arithmetic and copies ran while one was open for 9% of the time, Pallas kernels for 24%

profile of v1, /device:TPU:0, one launch (start us, length us, event | category | flops | bytes accessed | tf_op | source)
XLA Modules:
  0.0 127.1 jit_solution(5147447341970642655)
XLA Ops:
  1.3 1.0 slice.121
  2.3 1.7 %collective-permute-start = (bf16[128,1280]{1,0:T(8,128)(2,1)S(1)}, bf16[128,1280]{1,0:T(8,128)(2,1)S(1)}, u32[]{:S(2)}, u32[]{:S(2)}) collective-permute-start(bf16[128,1280]{1,0:T(8,128)(2,1)S(1)} %slice.121), channel_id=1, source_target_pairs={{0,64},{32,96},{64,0},{96,32},{1,65},{33,97},{65,1},{97,33},{2,66}... | collective-permute-start | bytes 983048 | tf_op jit(solution)/shard_map/ppermute | solution.py:342
  4.1 2.0 %copy.25.dino = bf16[2,36,36,384]{3,2,1,0:T(8,128)(2,1)S(1)} copy(bf16[2,36,36,384]{3,0,2,1:T(2,128)(2,1)} %param.11) | data formatting | bytes 3981312 | tf_op args[1]
  6.6 1.0 copy-done.14
  7.6 3.6 %targets.1 = (bf16[2,2,256,1152]{3,2,1,0:T(8,128)(2,1)S(1)}, bf16[2,2,256,1152]{3,2,1,0:T(8,128)(2,1)S(1)}) custom-call(s32[4]{0:T(128)S(1)} %pad_add_fusion.order_ref, bf16[2,36,36,384]{3,2,1,0:T(8,128)(2,1)S(1)} %copy.25.dino, bf16[2,36,36,288]{3,2,1,0:T(8,128)(2,1)S(1)} %copy.26.siglip, bf16[2,32,32,320]{3,2,1,0:T(8,128)(2,1)S(1)} %copy-done.14), custom_call_target="tpu_custom_call" | custom-call | flops 1000 | bytes 1000 | tf_op jit(solution)/shard_map/targets/pallas_call | solution.py:87
  11.2 1.4 %copy-done = bf16[2,2,256,1152]{3,2,1,0:T(8,128)(2,1)} copy-done((bf16[2,2,256,1152]{3,2,1,0:T(8,128)(2,1)}, bf16[2,2,256,1152]{3,2,1,0:T(8,128)(2,1)S(1)}, u32[]{:S(2)}) %copy-start) | copy-done | bytes 2359320
  12.6 1.0 copy-done.7
  13.8 1.6 %collective-permute-start.4 = (bf16[384,1280]{1,0:T(8,128)(2,1)S(1)}, bf16[384,1280]{1,0:T(8,128)(2,1)S(1)}, u32[]{:S(2)}, u32[]{:S(2)}) collective-permute-start(bf16[384,1280]{1,0:T(8,128)(2,1)S(1)} %slice.122), channel_id=1, source_target_pairs={{0,64},{32,96},{64,0},{96,32},{1,65},{33,97},{65,1},{97,33},{2,66}... | collective-permute-start | bytes 2949128 | tf_op jit(solution)/shard_map/ppermute | solution.py:342
  15.4 2.7 %collective-permute-done.5.refs_2_.refs_3_ = bf16[1024,1152]{1,0:T(8,128)(2,1)S(1)} collective-permute-done((bf16[1024,1152]{1,0:T(8,128)(2,1)S(1)}, bf16[1024,1152]{1,0:T(8,128)(2,1)S(1)}, u32[]{:S(2)}, u32[]{:S(2)}) %collective-permute-start.5) | collective-permute-done | bytes 2359328 | tf_op jit(solution)/shard_map/ppermute | solution.py:350
  18.1 1.4 %copy-done.2 = bf16[1024,1152]{1,0:T(8,128)(2,1)} copy-done((bf16[1024,1152]{1,0:T(8,128)(2,1)}, bf16[1024,1152]{1,0:T(8,128)(2,1)S(1)}, u32[]{:S(2)}) %copy-start.2) | copy-done | bytes 2359320
  19.5 1.1 copy-done.8
  20.7 15.1 %adapt.3 = (bf16[1024,768]{1,0:T(8,128)(2,1)S(1)}, bf16[1024,1536]{1,0:T(8,128)(2,1)}, f32[1024,768]{1,0:T(8,128)}, f32[8,1024]{1,0:T(8,128)S(1)}, bf16[1024,768...) custom-call(bf16[512,1280]{1,0:T(8,128)(2,1)S(1)} %bitcast.26, ...), custom_call_target="tpu_custom_call" | custom-call | flops 1000 | bytes 1000 | tf_op jit(solution)/shard_map/adapt/pallas_call | solution.py:259
  35.8 2.3 %collective-permute-done.4.refs_1_ = bf16[384,1280]{1,0:T(8,128)(2,1)S(1)} collective-permute-done((bf16[384,1280]{1,0:T(8,128)(2,1)S(1)}, bf16[384,1280]{1,0:T(8,128)(2,1)S(1)}, u32[]{:S(2)}, u32[]{:S(2)}) %collective-permute-start.4) | collective-permute-done | bytes 983072 | tf_op jit(solution)/shard_map/ppermute | solution.py:342
  38.1 1.7 %copy-done.3 = bf16[1024,1152]{1,0:T(8,128)(2,1)S(1)} copy-done((bf16[1024,1152]{1,0:T(8,128)(2,1)S(1)}, bf16[1024,1152]{1,0:T(8,128)(2,1)}, u32[]{:S(2)}) %copy-start.3) | copy-done | bytes 2359320
  39.8 7.8 %adapt.4 = (bf16[1024,768]{1,0:T(8,128)(2,1)S(1)}, bf16[1024,1536]{1,0:T(8,128)(2,1)}, f32[1024,768]{1,0:T(8,128)}, f32[8,1024]{1,0:T(8,128)S(1)}) custom-call(bf16[128,1280]{1,0:T(8,128)(2,1)S(1)} %collective-permute-done.refs_0_, ...), custom_call_target="tpu_custom_call", output_to_operand_aliasing={{0}: (7, {}), {1}: (8, {}), {2}: (9, {}), {3}: (10, {})} | custom-call | flops 1000 | bytes 1000 | tf_op jit(solution)/shard_map/adapt/pallas_call | solution.py:259
  47.6 1.6 %collective-permute-start.6 = (f32[8,1024]{1,0:T(8,128)S(1)}, f32[8,1024]{1,0:T(8,128)S(1)}, u32[]{:S(2)}, u32[]{:S(2)}) collective-permute-start(f32[8,1024]{1,0:T(8,128)S(1)} %get-tuple-element.54), channel_id=1, source_target_pairs={{0,64},{32,96},{64,0},{96,32},{1,65},{33,97},{65,1},{97,33},{2,66}... | collective-permute-start | bytes 98312 | tf_op jit(solution)/shard_map/ppermute | solution.py:366
  49.2 11.4 %adapt.5 = (bf16[1024,768]{1,0:T(8,128)(2,1)S(1)}, bf16[1024,1280]{1,0:T(8,128)(2,1)}, f32[1024,768]{1,0:T(8,128)}, f32[8,1024]{1,0:T(8,128)S(1)}, bf16[1024,768...) custom-call(bf16[128,1280]{1,0:T(8,128)(2,1)S(1)} %collective-permut, ...), custom_call_target="tpu_custom_call", output_to_operand_aliasing={{0}: (10, {}), {1}: (11, {}), {2}: (12, {}), {3}: (13, {}),... | custom-call | flops 1000 | bytes 1000 | tf_op jit(solution)/shard_map/adapt/pallas_call | solution.py:259
  61.2 1.5 %collective-permute-start.10 = (f32[8,1024]{1,0:T(8,128)S(1)}, f32[8,1024]{1,0:T(8,128)S(1)}, u32[]{:S(2)}, u32[]{:S(2)}) collective-permute-start(f32[8,1024]{1,0:T(8,128)S(1)} %get-tuple-element.76), channel_id=1, source_target_pairs={{0,64},{32,96},{64,0},{96,32},{1,65},{33,97},{65,1},{97,33},{2,66}... | collective-permute-start | bytes 98312 | tf_op jit(solution)/shard_map/ppermute | solution.py:366
  62.8 2.9 %convolution_convert_fusion.dino = bf16[1536,768]{1,0:T(8,128)(2,1)S(1)} fusion(bf16[1024,1536]{1,0:T(8,128)(2,1)S(1)} %copy-done.17, f32[1024,768]{1,0:T(8,128)S(1)} %copy-done.18, bf16[1024,768]{1,0:T(8,128)(2,1)S(1)} %get-tuple-element.67, f32[1024]{0:T(1024)S(1)} %get-tuple-element.68, f32[1024]{0:T(1024)S(1)} %get-tuple-element.66), kind=kOutput, calls=%fused_computation.1 | convolution fusion | flops 2421030912 | bytes 10231808 | tf_op jit(solution)/shard_map/tk,tc->kc/dot_general | solution.py:374
  66.3 2.5 %convolution_convert_fusion.2.sam = bf16[1280,768]{1,0:T(8,128)(2,1)S(1)} fusion(bf16[1024,1280]{1,0:T(8,128)(2,1)S(1)} %copy-done.19, f32[1024,768]{1,0:T(8,128)S(1)} %copy-done.15, bf16[1024,768]{1,0:T(8,128)(2,1)S(1)} %get-tuple-element.72, f32[1024]{0:T(1024)S(1)} %get-tuple-element.73, f32[1024]{0:T(1024)S(1)} %get-tuple-element.71), kind=kOutput, calls=%fused_computation.3 | convolution fusion | flops 2018181120 | bytes 9314304 | tf_op jit(solution)/shard_map/tk,tc->kc/dot_general | solution.py:374
  69.6 2.3 %convolution_convert_fusion.1.siglip = bf16[1152,768]{1,0:T(8,128)(2,1)S(1)} fusion(bf16[1024,1152]{1,0:T(8,128)(2,1)S(1)} %get-tuple-element.75, f32[1024,768]{1,0:T(8,128)S(1)} %copy-done.16, bf16[1024,768]{1,0:T(8,128)(2,1)S(1)} %get-tuple-element.78, f32[1024]{0:T(1024)S(1)} %get-tuple-element.79, f32[1024]{0:T(1024)S(1)} %get-tuple-element.77), kind=kOutput, calls=%fused_computation.2 | convolution fusion | flops 1816756224 | bytes 8855552 | tf_op jit(solution)/shard_map/tk,tc->kc/dot_general | solution.py:374
  72.1 2.4 %collective-permute-done.11.siglip_other = bf16[1152,384]{1,0:T(8,128)(2,1)S(1)} collective-permute-done((bf16[1152,384]{1,0:T(8,128)(2,1)S(1)}, bf16[1152,384]{1,0:T(8,128)(2,1)S(1)}, u32[]{:S(2)}, u32[]{:S(2)}) %collective-permute-start.11) | collective-permute-done | bytes 884768 | tf_op jit(solution)/shard_map/ppermute | solution.py:383
  74.5 1.6 %pack.1 = bf16[32,352,128]{2,1,0:T(8,128)(2,1)S(1)} custom-call(bf16[1536,768]{1,0:T(8,128)(2,1)S(1)} %convolution_convert_fusion.dino, bf16[1536,384]{1,0:T(8,128)(2,1)S(1)} %collective-permute-done.7.dino_other, bf16[1280,768]{1,0:T(8,128)(2,1)S(1)} %convolution_convert_fusion.2.sam, bf16[1280,384]{1,0:T(8,128)(2,1)S(1)} %collective-permute-done.9.sam_other, ...), custom_call_target="tpu_custom_call" | custom-call | tf_op jit(solution)/shard_map/pack/pallas_call | solution.py:299
  76.2 48.5 %all_to_all.5 = bf16[32,352,128]{2,1,0:T(8,128)(2,1)S(1)} all-to-all(bf16[32,352,128]{2,1,0:T(8,128)(2,1)S(1)} %pack.1), channel_id=1, replica_groups=mesh['grp'=4,'dp'=32] {'dp'}, dimensions={0} | all-to-all | bytes 5767168 | tf_op jit(solution)/shard_map/all_to_all | solution.py:384
  (80 shorter events, 6.0 us)
Async XLA Ops:
  0.6 12.9 %collective-permute-start.1 = (bf16[1536,384]{1,0:T(8,128)(2,1)}, bf16[1536,384]{1,0:T(8,128)(2,1)S(1)}, u32[]{:S(2)}, u32[]{:S(2)}) collective-permute-start(bf16[1536,384]{1,0:T(8,128)(2,1)} %refs_5_.1), channel_id=1, source_target_pairs={{0,32},{32,0},{64,96},{96,64},{1,33},{33,1},{65,97},{97,65},{2,34}... | collective-permute-start | bytes 3538952 | tf_op jit(solution)/shard_map/ppermute | solution.py:345
  0.7 11.9 %collective-permute-start.2 = (bf16[320,1280]{1,0:T(8,128)(2,1)}, bf16[320,1280]{1,0:T(8,128)(2,1)S(1)}, u32[]{:S(2)}, u32[]{:S(2)}) collective-permute-start(bf16[320,1280]{1,0:T(8,128)(2,1)} %bitcast.27), channel_id=1, source_target_pairs={{0,32},{32,0},{64,96},{96,64},{1,33},{33,1},{65,97},{97,65},{2,34}... | collective-permute-start | bytes 2457608 | tf_op jit(solution)/shard_map/ppermute | solution.py:345
  1.2 11.4 %collective-permute-start.3 = (bf16[288,1152]{1,0:T(8,128)(2,1)}, bf16[288,1152]{1,0:T(8,128)(2,1)}, u32[]{:S(2)}, u32[]{:S(2)}) collective-permute-start(bf16[288,1152]{1,0:T(8,128)(2,1)} %bitcast.30), channel_id=1, source_target_pairs={{0,32},{32,0},{64,96},{96,64},{1,33},{33,1},{65,97},{97,65},{2,34}... | collective-permute-start | bytes 1990664 | tf_op jit(solution)/shard_map/ppermute | solution.py:345
  2.3 10.3 %collective-permute-start = (bf16[128,1280]{1,0:T(8,128)(2,1)S(1)}, bf16[128,1280]{1,0:T(8,128)(2,1)S(1)}, u32[]{:S(2)}, u32[]{:S(2)}) collective-permute-start(bf16[128,1280]{1,0:T(8,128)(2,1)S(1)} %slice.121), channel_id=1, source_target_pairs={{0,64},{32,96},{64,0},{96,32},{1,65},{33,97},{65,1},{97,33},{2,66}... | collective-permute-start | bytes 983048 | tf_op jit(solution)/shard_map/ppermute | solution.py:342
  7.6 6.1 %copy-start.4 = (bf16[2,8,32,1280]{3,2,1,0:T(8,128)(2,1)S(1)}, bf16[2,8,32,1280]{3,2,1,0:T(8,128)(2,1)}, u32[]{:S(2)}) copy-start(bf16[2,8,32,1280]{3,2,1,0:T(8,128)(2,1)} %param.10) | copy-start | bytes 3932164
  7.6 11.9 %copy-start.5 = (bf16[1536,384]{1,0:T(8,128)(2,1)S(1)}, bf16[1536,384]{1,0:T(8,128)(2,1)}, u32[]{:S(2)}) copy-start(bf16[1536,384]{1,0:T(8,128)(2,1)} %refs_5_.1) | copy-start | bytes 3538948
  7.6 11.9 %copy-start.6 = (bf16[1280,320]{0,1:T(8,128)(2,1)S(1)}, bf16[1280,320]{0,1:T(8,128)(2,1)}, u32[]{:S(2)}) copy-start(bf16[1280,320]{0,1:T(8,128)(2,1)} %param.19) | copy-start | bytes 2457604
  7.6 11.9 %copy-start.10 = (bf16[1152,288]{0,1:T(8,128)(2,1)S(1)}, bf16[1152,288]{0,1:T(8,128)(2,1)}, u32[]{:S(2)}) copy-start(bf16[1152,288]{0,1:T(8,128)(2,1)} %param.17) | copy-start | bytes 1990660
  13.6 4.5 %collective-permute-start.5 = (bf16[1024,1152]{1,0:T(8,128)(2,1)S(1)}, bf16[1024,1152]{1,0:T(8,128)(2,1)S(1)}, u32[]{:S(2)}, u32[]{:S(2)}) collective-permute-start(bf16[1024,1152]{1,0:T(8,128)(2,1)S(1)} %bitcast.33), channel_id=1, source_target_pairs={{0,32},{32,0},{64,96},{96,64},{1,33},{33,1},{65,97},{97,65},{2,34}... | collective-permute-start | bytes 7077896 | tf_op jit(solution)/shard_map/ppermute | solution.py:350
  13.8 24.3 %collective-permute-start.4 = (bf16[384,1280]{1,0:T(8,128)(2,1)S(1)}, bf16[384,1280]{1,0:T(8,128)(2,1)S(1)}, u32[]{:S(2)}, u32[]{:S(2)}) collective-permute-start(bf16[384,1280]{1,0:T(8,128)(2,1)S(1)} %slice.122), channel_id=1, source_target_pairs={{0,64},{32,96},{64,0},{96,32},{1,65},{33,97},{65,1},{97,33},{2,66}... | collective-permute-start | bytes 2949128 | tf_op jit(solution)/shard_map/ppermute | solution.py:342
  20.7 17.4 %copy-start.1 = (bf16[2,2,256,1152]{3,2,1,0:T(8,128)(2,1)S(1)}, bf16[2,2,256,1152]{3,2,1,0:T(8,128)(2,1)}, u32[]{:S(2)}) copy-start(bf16[2,2,256,1152]{3,2,1,0:T(8,128)(2,1)} %copy-done) | copy-start | bytes 7077892
  39.7 9.4 %copy-start.9 = (bf16[320,1280]{1,0:T(8,128)(2,1)S(1)}, bf16[320,1280]{1,0:T(8,128)(2,1)}, u32[]{:S(2)}) copy-start(bf16[320,1280]{1,0:T(8,128)(2,1)} %copy-done.7) | copy-start | bytes 2457604
  39.7 9.4 %copy-start.11 = (bf16[1152,288]{0,1:T(8,128)(2,1)S(1)}, bf16[1152,288]{0,1:T(8,128)(2,1)}, u32[]{:S(2)}) copy-start(bf16[1152,288]{0,1:T(8,128)(2,1)} %param.17) | copy-start | bytes 1990660
  39.7 9.4 %copy-start.12 = (bf16[1024,1152]{1,0:T(8,128)(2,1)S(1)}, bf16[1024,1152]{1,0:T(8,128)(2,1)}, u32[]{:S(2)}) copy-start(bf16[1024,1152]{1,0:T(8,128)(2,1)} %get-tuple-element.62.refs_15_) | copy-start | bytes 7077892
  39.8 9.4 %copy-start.13 = (bf16[1024,768]{1,0:T(8,128)(2,1)S(1)}, bf16[1024,768]{1,0:T(8,128)(2,1)}, u32[]{:S(2)}) copy-start(bf16[1024,768]{1,0:T(8,128)(2,1)} %get-tuple-element.61.refs_14_) | copy-start | bytes 4718596
  47.6 15.1 %collective-permute-start.6 = (f32[8,1024]{1,0:T(8,128)S(1)}, f32[8,1024]{1,0:T(8,128)S(1)}, u32[]{:S(2)}, u32[]{:S(2)}) collective-permute-start(f32[8,1024]{1,0:T(8,128)S(1)} %get-tuple-element.54), channel_id=1, source_target_pairs={{0,64},{32,96},{64,0},{96,32},{1,65},{33,97},{65,1},{97,33},{2,66}... | collective-permute-start | bytes 98312 | tf_op jit(solution)/shard_map/ppermute | solution.py:366
  49.2 13.6 %copy-start.17 = (bf16[1024,1536]{1,0:T(8,128)(2,1)S(1)}, bf16[1024,1536]{1,0:T(8,128)(2,1)}, u32[]{:S(2)}) copy-start(bf16[1024,1536]{1,0:T(8,128)(2,1)} %get-tuple-element.53) | copy-start | bytes 9437188
  49.2 13.6 %copy-start.18 = (f32[1024,768]{1,0:T(8,128)S(1)}, f32[1024,768]{1,0:T(8,128)}, u32[]{:S(2)}) copy-start(f32[1024,768]{1,0:T(8,128)} %get-tuple-element.69) | copy-start | bytes 9437188
  60.6 5.6 %collective-permute-start.8 = (f32[8,1024]{1,0:T(8,128)S(1)}, f32[8,1024]{1,0:T(8,128)S(1)}, u32[]{:S(2)}, u32[]{:S(2)}) collective-permute-start(f32[8,1024]{1,0:T(8,128)S(1)} %get-tuple-element.65), channel_id=1, source_target_pairs={{0,64},{32,96},{64,0},{96,32},{1,65},{33,97},{65,1},{97,33},{2,66}... | collective-permute-start | bytes 98312 | tf_op jit(solution)/shard_map/ppermute | solution.py:366
  61.2 8.3 %collective-permute-start.10 = (f32[8,1024]{1,0:T(8,128)S(1)}, f32[8,1024]{1,0:T(8,128)S(1)}, u32[]{:S(2)}, u32[]{:S(2)}) collective-permute-start(f32[8,1024]{1,0:T(8,128)S(1)} %get-tuple-element.76), channel_id=1, source_target_pairs={{0,64},{32,96},{64,0},{96,32},{1,65},{33,97},{65,1},{97,33},{2,66}... | collective-permute-start | bytes 98312 | tf_op jit(solution)/shard_map/ppermute | solution.py:366
  62.8 3.5 %copy-start.15 = (f32[1024,768]{1,0:T(8,128)S(1)}, f32[1024,768]{1,0:T(8,128)}, u32[]{:S(2)}) copy-start(f32[1024,768]{1,0:T(8,128)} %get-tuple-element.74) | copy-start | bytes 9437188
  65.9 8.7 %collective-permute-start.7 = (bf16[1536,384]{1,0:T(8,128)(2,1)S(1)}, bf16[1536,384]{1,0:T(8,128)(2,1)S(1)}, u32[]{:S(2)}, u32[]{:S(2)}) collective-permute-start(bf16[1536,384]{1,0:T(8,128)(2,1)S(1)} %slice.128), channel_id=1, source_target_pairs={{0,32},{32,0},{64,96},{96,64},{1,33},{33,1},{65,97},{97,65},{2,34}... | collective-permute-start | bytes 3538952 | tf_op jit(solution)/shard_map/ppermute | solution.py:383
  68.9 5.6 %collective-permute-start.9 = (bf16[1280,384]{1,0:T(8,128)(2,1)S(1)}, bf16[1280,384]{1,0:T(8,128)(2,1)S(1)}, u32[]{:S(2)}, u32[]{:S(2)}) collective-permute-start(bf16[1280,384]{1,0:T(8,128)(2,1)S(1)} %slice.134), channel_id=1, source_target_pairs={{0,32},{32,0},{64,96},{96,64},{1,33},{33,1},{65,97},{97,65},{2,34}... | collective-permute-start | bytes 2949128 | tf_op jit(solution)/shard_map/ppermute | solution.py:383
  72.0 2.5 %collective-permute-start.11 = (bf16[1152,384]{1,0:T(8,128)(2,1)S(1)}, bf16[1152,384]{1,0:T(8,128)(2,1)S(1)}, u32[]{:S(2)}, u32[]{:S(2)}) collective-permute-start(bf16[1152,384]{1,0:T(8,128)(2,1)S(1)} %slice.140), channel_id=1, source_target_pairs={{0,32},{32,0},{64,96},{96,64},{1,33},{33,1},{65,97},{97,65},{2,34}... | collective-permute-start | bytes 2654216 | tf_op jit(solution)/shard_map/ppermute | solution.py:383
  (9 other events, 16.9 us)

commit v2 on v1

--- a/solution.py
+++ b/solution.py
@@ -244,7 +244,6 @@
             pltpu.VMEM((8, rows), f32),
         ]
     n = len(teachers)
-    held = sum(math.prod(b.shape) * jnp.dtype(b.dtype).itemsize for b in scratch)
     scratch += [
         pltpu.SemaphoreType.DMA((5 * n + len(pieces),)),
         pltpu.SemaphoreType.DMA((4 * n,)),
@@ -263,7 +262,7 @@
         out_shape=outs,
         scratch_shapes=scratch,
         input_output_aliases=aliases,
-        compiler_params=pltpu.CompilerParams(vmem_limit_bytes=max(held + 3 * MIB, 44 * MIB)),
+        compiler_params=pltpu.CompilerParams(vmem_limit_bytes=44 * MIB),
         cost_estimate=pl.CostEstimate(flops=1000, bytes_accessed=1000, transcendentals=0),
         name="adapt",
     )(*args)
@@ -278,12 +277,10 @@
     tall = rows[1]
     for j in range(blocks):
         d, m, s = [total[j * r : (j + 1) * r] for total, r in zip(sums, rows)]
-        s = jnp.concatenate([s, jnp.zeros((tall - rows[2], HALF), f32)], axis=0)
-        mixed = m[:, 256:] + pltpu.roll(s[:, 256:], 64, 1)
+        last = jnp.concatenate([s[:, 256:], jnp.zeros((tall - rows[2], 128), f32)], axis=0)
+        mixed = m[:, 256:] + pltpu.roll(last, 64, 1)
         strips = [d[:, :128], d[:, 128:256], d[:, 256:], m[:, :128], m[:, 128:256], mixed]
         strips += [s[:, :128], s[:, 128:256]]
-        count = sum(strip.shape[0] for strip in strips)
-        strips.append(jnp.zeros((out.shape[1] - count, 128), f32))
         out[j] = jnp.concatenate(strips, axis=0).astype(bf16)
 
 
@@ -291,7 +288,7 @@
     blocks = 4
     steps = n_dp // blocks
     rows = [g.shape[0] // n_dp for g in grads]
-    height = -(-(3 * rows[0] + 5 * rows[1]) // 16) * 16
+    height = 3 * rows[0] + 3 * rows[1] + 2 * rows[2]
     args, specs = [], []
     for grad, other, r in zip(grads, received, rows):
         args += [grad, other]
@@ -307,16 +304,33 @@
     )(*args)
 
 
-def unpack(total, rows):
-    dino, sam, siglip = rows
-    at = 3 * dino
-    mixed = total[at + 2 * sam : at + 3 * sam]
-    low = at + 3 * sam
-    return (
-        jnp.concatenate([total[i * dino : (i + 1) * dino] for i in range(3)], axis=1),
-        jnp.concatenate([total[low : low + siglip], total[low + sam : low + sam + siglip], mixed[:siglip, 64:96]], axis=1),
-        jnp.concatenate([total[at : at + sam], total[at + sam : at + 2 * sam], mixed[:, :64]], axis=1),
-    )
+def unpack_kernel(split, dino, siglip, sam):
+    total = split[0].astype(f32)
+    for i in range(1, split.shape[0]):
+        total += split[i].astype(f32)
+    at = 0
+    for out, strips in ((dino, 3), (sam, 2)):
+        rows = out.shape[0]
+        for i in range(strips):
+            out[:, 128 * i : 128 * (i + 1)] = total[at : at + rows]
+            at += rows
+    mixed = total[at : at + sam.shape[0]]
+    sam[:, 256:] = mixed[:, : sam.shape[1] - 256]
+    siglip[:, 256:] = pltpu.roll(mixed, 64, 1)[: siglip.shape[0], : siglip.shape[1] - 256]
+    at += sam.shape[0]
+    for i in range(2):
+        rows = siglip.shape[0]
+        siglip[:, 128 * i : 128 * (i + 1)] = total[at : at + rows]
+        at += rows
+
+
+def unpack(split, shapes):
+    return pl.pallas_call(
+        unpack_kernel,
+        out_shape=[jax.ShapeDtypeStruct(shape, f32) for shape in shapes],
+        compiler_params=pltpu.CompilerParams(vmem_limit_bytes=16 * MIB),
+        name="unpack",
+    )(split)
 
 
 def shards(
@@ -382,9 +396,8 @@
     grads.append(gradient(siglip_state, grads[1]))
     received = [lax.ppermute(grad[:, HALF:], "grp", CORE) for grad in grads]
     split = lax.all_to_all(pack(grads, received, n_dp), "dp", 0, 0, tiled=True)
-    return unpack(
-        jnp.sum(split.astype(f32), axis=0), [w.shape[0] // n_dp for w in (w2_dino, w2_sam, w2_siglip)]
-    )
+    shapes = [(w.shape[0] // n_dp, w.shape[1]) for w in (w2_dino, w2_siglip, w2_sam)]
+    return tuple(unpack(split, shapes))
 
 
 def solution(mesh):

time: 127 us -> 125 us (0.984)
  other arithmetic: 2.52 us -> 0.23 us
    concatenate x3 -> x0, other arithmetic: 1.9 us -> none  [the longest x1 0.64 us: unpack(): jnp.concatenate([total[i * dino:(i + 1) * dino] for i in range(3)], axis=1)]
where the time goes in v2:
time: 125 us
  blocking collectives  47.4 us (38%)
  Pallas kernels  40.6 us (32%)
  local copies, waits for them, and re-layouts  11.5 us (9%)
  starting transfers between devices  8.88 us (7%)
  matrix products  7.71 us (6%)
  waiting for transfers between devices  7.4 us (6%)
    all_to_all x1, blocking collectives, shards(): split = lax.all_to_all(pack(grads, received, n_dp), 'dp', 0, 0, tiled=True)  47.4 us
    pallas_call x3, Pallas kernels, adapt(): pl.pallas_call(functools.partial(adapt_kernel, which, prior is None, turn...  34.3 us
    unnamed x44, local copies, waits for them, and re-layouts  10.1 us
    dot_general x3, matrix products, gradient(): grad = jnp.einsum('tk,tc->kc', hidden, error, preferred_element_type=f32)  7.71 us
    ppermute x3, starting transfers between devices, gradient(): sums = part + jnp.roll(lax.ppermute(part, 'grp', CHIP), own_tokens, axis=1)  3.68 us
    pallas_call x1, Pallas kernels, targets(): pl.pallas_call(targets_kernel, grid_spec=pltpu.PrefetchScalarGridSpec(num...  3.56 us
    ppermute x2, starting transfers between devices, shards(): lax.ppermute(piece, 'grp', CHIP)  3.36 us
    ppermute x1, waiting for transfers between devices, shards(): goals = (kept, lax.ppermute(sent, 'grp', CORE))  2.7 us
  transfers between devices with their start and end apart: 12, of which 3 were waited for; matrix products, arithmetic and copies ran while one was open for 9% of the time, Pallas kernels for 24%

profile of v2, /device:TPU:0, one launch (start us, length us, event | category | flops | bytes accessed | tf_op | source)
XLA Modules:
  0.0 124.6 jit_solution(13350375771570662442)
XLA Ops:
  1.3 1.0 slice.82
  2.3 1.7 %collective-permute-start = (bf16[128,1280]{1,0:T(8,128)(2,1)S(1)}, bf16[128,1280]{1,0:T(8,128)(2,1)S(1)}, u32[]{:S(2)}, u32[]{:S(2)}) collective-permute-start(bf16[128,1280]{1,0:T(8,128)(2,1)S(1)} %slice.82), channel_id=1, source_target_pairs={{0,64},{32,96},{64,0},{96,32},{1,65},{33,97},{65,1},{97,33},{2,66}... | collective-permute-start | bytes 983048 | tf_op jit(solution)/shard_map/ppermute | solution.py:356
  4.1 2.0 %copy.25.dino = bf16[2,36,36,384]{3,2,1,0:T(8,128)(2,1)S(1)} copy(bf16[2,36,36,384]{3,0,2,1:T(2,128)(2,1)} %param.11) | data formatting | bytes 3981312 | tf_op args[1]
  6.6 1.0 copy-done.14
  7.6 3.6 %targets.1 = (bf16[2,2,256,1152]{3,2,1,0:T(8,128)(2,1)S(1)}, bf16[2,2,256,1152]{3,2,1,0:T(8,128)(2,1)S(1)}) custom-call(s32[4]{0:T(128)S(1)} %pad_add_fusion.order_ref, bf16[2,36,36,384]{3,2,1,0:T(8,128)(2,1)S(1)} %copy.25.dino, bf16[2,36,36,288]{3,2,1,0:T(8,128)(2,1)S(1)} %copy.26.siglip, bf16[2,32,32,320]{3,2,1,0:T(8,128)(2,1)S(1)} %copy-done.14), custom_call_target="tpu_custom_call" | custom-call | flops 1000 | bytes 1000 | tf_op jit(solution)/shard_map/targets/pallas_call | solution.py:87
  11.2 1.4 %copy-done = bf16[2,2,256,1152]{3,2,1,0:T(8,128)(2,1)} copy-done((bf16[2,2,256,1152]{3,2,1,0:T(8,128)(2,1)}, bf16[2,2,256,1152]{3,2,1,0:T(8,128)(2,1)S(1)}, u32[]{:S(2)}) %copy-start) | copy-done | bytes 2359320
  13.8 1.6 %collective-permute-start.4 = (bf16[384,1280]{1,0:T(8,128)(2,1)S(1)}, bf16[384,1280]{1,0:T(8,128)(2,1)S(1)}, u32[]{:S(2)}, u32[]{:S(2)}) collective-permute-start(bf16[384,1280]{1,0:T(8,128)(2,1)S(1)} %slice.83), channel_id=1, source_target_pairs={{0,64},{32,96},{64,0},{96,32},{1,65},{33,97},{65,1},{97,33},{2,66}... | collective-permute-start | bytes 2949128 | tf_op jit(solution)/shard_map/ppermute | solution.py:356
  15.4 2.7 %collective-permute-done.5.refs_2_.refs_3_ = bf16[1024,1152]{1,0:T(8,128)(2,1)S(1)} collective-permute-done((bf16[1024,1152]{1,0:T(8,128)(2,1)S(1)}, bf16[1024,1152]{1,0:T(8,128)(2,1)S(1)}, u32[]{:S(2)}, u32[]{:S(2)}) %collective-permute-start.5) | collective-permute-done | bytes 2359328 | tf_op jit(solution)/shard_map/ppermute | solution.py:364
  18.1 1.4 %copy-done.2 = bf16[1024,1152]{1,0:T(8,128)(2,1)} copy-done((bf16[1024,1152]{1,0:T(8,128)(2,1)}, bf16[1024,1152]{1,0:T(8,128)(2,1)S(1)}, u32[]{:S(2)}) %copy-start.2) | copy-done | bytes 2359320
  19.5 1.1 copy-done.8
  20.7 15.1 %adapt.3 = (bf16[1024,768]{1,0:T(8,128)(2,1)S(1)}, bf16[1024,1536]{1,0:T(8,128)(2,1)}, f32[1024,768]{1,0:T(8,128)}, f32[8,1024]{1,0:T(8,128)S(1)}, bf16[1024,768...) custom-call(bf16[512,1280]{1,0:T(8,128)(2,1)S(1)} %bitcast.26, ...), custom_call_target="tpu_custom_call" | custom-call | flops 1000 | bytes 1000 | tf_op jit(solution)/shard_map/adapt/pallas_call | solution.py:258
  35.8 2.3 %collective-permute-done.4.refs_1_ = bf16[384,1280]{1,0:T(8,128)(2,1)S(1)} collective-permute-done((bf16[384,1280]{1,0:T(8,128)(2,1)S(1)}, bf16[384,1280]{1,0:T(8,128)(2,1)S(1)}, u32[]{:S(2)}, u32[]{:S(2)}) %collective-permute-start.4) | collective-permute-done | bytes 983072 | tf_op jit(solution)/shard_map/ppermute | solution.py:356
  38.1 1.7 %copy-done.3 = bf16[1024,1152]{1,0:T(8,128)(2,1)S(1)} copy-done((bf16[1024,1152]{1,0:T(8,128)(2,1)S(1)}, bf16[1024,1152]{1,0:T(8,128)(2,1)}, u32[]{:S(2)}) %copy-start.3) | copy-done | bytes 2359320
  39.7 7.8 %adapt.4 = (bf16[1024,768]{1,0:T(8,128)(2,1)S(1)}, bf16[1024,1536]{1,0:T(8,128)(2,1)}, f32[1024,768]{1,0:T(8,128)}, f32[8,1024]{1,0:T(8,128)S(1)}) custom-call(bf16[128,1280]{1,0:T(8,128)(2,1)S(1)} %collective-permute-done.refs_0_, ...), custom_call_target="tpu_custom_call", output_to_operand_aliasing={{0}: (7, {}), {1}: (8, {}), {2}: (9, {}), {3}: (10, {})} | custom-call | flops 1000 | bytes 1000 | tf_op jit(solution)/shard_map/adapt/pallas_call | solution.py:258
  47.6 1.6 %collective-permute-start.6 = (f32[8,1024]{1,0:T(8,128)S(1)}, f32[8,1024]{1,0:T(8,128)S(1)}, u32[]{:S(2)}, u32[]{:S(2)}) collective-permute-start(f32[8,1024]{1,0:T(8,128)S(1)} %get-tuple-element.54), channel_id=1, source_target_pairs={{0,64},{32,96},{64,0},{96,32},{1,65},{33,97},{65,1},{97,33},{2,66}... | collective-permute-start | bytes 98312 | tf_op jit(solution)/shard_map/ppermute | solution.py:380
  49.2 11.4 %adapt.5 = (bf16[1024,768]{1,0:T(8,128)(2,1)S(1)}, bf16[1024,1280]{1,0:T(8,128)(2,1)}, f32[1024,768]{1,0:T(8,128)}, f32[8,1024]{1,0:T(8,128)S(1)}, bf16[1024,768...) custom-call(bf16[128,1280]{1,0:T(8,128)(2,1)S(1)} %collective-permut, ...), custom_call_target="tpu_custom_call", output_to_operand_aliasing={{0}: (10, {}), {1}: (11, {}), {2}: (12, {}), {3}: (13, {}),... | custom-call | flops 1000 | bytes 1000 | tf_op jit(solution)/shard_map/adapt/pallas_call | solution.py:258
  61.2 1.5 %collective-permute-start.10 = (f32[8,1024]{1,0:T(8,128)S(1)}, f32[8,1024]{1,0:T(8,128)S(1)}, u32[]{:S(2)}, u32[]{:S(2)}) collective-permute-start(f32[8,1024]{1,0:T(8,128)S(1)} %get-tuple-element.76), channel_id=1, source_target_pairs={{0,64},{32,96},{64,0},{96,32},{1,65},{33,97},{65,1},{97,33},{2,66}... | collective-permute-start | bytes 98312 | tf_op jit(solution)/shard_map/ppermute | solution.py:380
  62.8 2.9 %convolution_convert_fusion.dino = bf16[1536,768]{1,0:T(8,128)(2,1)S(1)} fusion(bf16[1024,1536]{1,0:T(8,128)(2,1)S(1)} %copy-done.17, f32[1024,768]{1,0:T(8,128)S(1)} %copy-done.18, bf16[1024,768]{1,0:T(8,128)(2,1)S(1)} %get-tuple-element.67, f32[1024]{0:T(1024)S(1)} %get-tuple-element.68, f32[1024]{0:T(1024)S(1)} %get-tuple-element.66), kind=kOutput, calls=%fused_computation | convolution fusion | flops 2421030912 | bytes 10231808 | tf_op jit(solution)/shard_map/tk,tc->kc/dot_general | solution.py:388
  66.3 2.5 %convolution_convert_fusion.2.sam = bf16[1280,768]{1,0:T(8,128)(2,1)S(1)} fusion(bf16[1024,1280]{1,0:T(8,128)(2,1)S(1)} %copy-done.19, f32[1024,768]{1,0:T(8,128)S(1)} %copy-done.15, bf16[1024,768]{1,0:T(8,128)(2,1)S(1)} %get-tuple-element.72, f32[1024]{0:T(1024)S(1)} %get-tuple-element.73, f32[1024]{0:T(1024)S(1)} %get-tuple-element.71), kind=kOutput, calls=%fused_computation.2 | convolution fusion | flops 2018181120 | bytes 9314304 | tf_op jit(solution)/shard_map/tk,tc->kc/dot_general | solution.py:388
  69.5 2.3 %convolution_convert_fusion.1.siglip = bf16[1152,768]{1,0:T(8,128)(2,1)S(1)} fusion(bf16[1024,1152]{1,0:T(8,128)(2,1)S(1)} %get-tuple-element.75, f32[1024,768]{1,0:T(8,128)S(1)} %copy-done.16, bf16[1024,768]{1,0:T(8,128)(2,1)S(1)} %get-tuple-element.78, f32[1024]{0:T(1024)S(1)} %get-tuple-element.79, f32[1024]{0:T(1024)S(1)} %get-tuple-element.77), kind=kOutput, calls=%fused_computation.1 | convolution fusion | flops 1816756224 | bytes 8855552 | tf_op jit(solution)/shard_map/tk,tc->kc/dot_general | solution.py:388
  72.1 2.4 %collective-permute-done.11.siglip_other = bf16[1152,384]{1,0:T(8,128)(2,1)S(1)} collective-permute-done((bf16[1152,384]{1,0:T(8,128)(2,1)S(1)}, bf16[1152,384]{1,0:T(8,128)(2,1)S(1)}, u32[]{:S(2)}, u32[]{:S(2)}) %collective-permute-start.11) | collective-permute-done | bytes 884768 | tf_op jit(solution)/shard_map/ppermute | solution.py:397
  74.5 1.6 %pack.1 = bf16[32,336,128]{2,1,0:T(8,128)(2,1)S(1)} custom-call(bf16[1536,768]{1,0:T(8,128)(2,1)S(1)} %convolution_convert_fusion.dino, bf16[1536,384]{1,0:T(8,128)(2,1)S(1)} %collective-permute-done.7.dino_other, bf16[1280,768]{1,0:T(8,128)(2,1)S(1)} %convolution_convert_fusion.2.sam, bf16[1280,384]{1,0:T(8,128)(2,1)S(1)} %collective-permute-done.9.sam_other, ...), custom_call_target="tpu_custom_call" | custom-call | tf_op jit(solution)/shard_map/pack/pallas_call | solution.py:296
  76.1 47.4 %all_to_all.5.split = bf16[32,336,128]{2,1,0:T(8,128)(2,1)S(1)} all-to-all(bf16[32,336,128]{2,1,0:T(8,128)(2,1)S(1)} %pack.1), channel_id=1, replica_groups=mesh['grp'=4,'dp'=32] {'dp'}, dimensions={0} | all-to-all | bytes 5505024 | tf_op jit(solution)/shard_map/all_to_all | solution.py:398
  123.5 1.1 unpack.1
  (72 shorter events, 4.5 us)
Async XLA Ops:
  0.6 12.9 %collective-permute-start.1 = (bf16[1536,384]{1,0:T(8,128)(2,1)}, bf16[1536,384]{1,0:T(8,128)(2,1)S(1)}, u32[]{:S(2)}, u32[]{:S(2)}) collective-permute-start(bf16[1536,384]{1,0:T(8,128)(2,1)} %refs_5_.1), channel_id=1, source_target_pairs={{0,32},{32,0},{64,96},{96,64},{1,33},{33,1},{65,97},{97,65},{2,34}... | collective-permute-start | bytes 3538952 | tf_op jit(solution)/shard_map/ppermute | solution.py:359
  0.7 11.9 %collective-permute-start.2 = (bf16[320,1280]{1,0:T(8,128)(2,1)}, bf16[320,1280]{1,0:T(8,128)(2,1)S(1)}, u32[]{:S(2)}, u32[]{:S(2)}) collective-permute-start(bf16[320,1280]{1,0:T(8,128)(2,1)} %bitcast.27), channel_id=1, source_target_pairs={{0,32},{32,0},{64,96},{96,64},{1,33},{33,1},{65,97},{97,65},{2,34}... | collective-permute-start | bytes 2457608 | tf_op jit(solution)/shard_map/ppermute | solution.py:359
  1.2 11.4 %collective-permute-start.3 = (bf16[288,1152]{1,0:T(8,128)(2,1)}, bf16[288,1152]{1,0:T(8,128)(2,1)}, u32[]{:S(2)}, u32[]{:S(2)}) collective-permute-start(bf16[288,1152]{1,0:T(8,128)(2,1)} %bitcast.30), channel_id=1, source_target_pairs={{0,32},{32,0},{64,96},{96,64},{1,33},{33,1},{65,97},{97,65},{2,34}... | collective-permute-start | bytes 1990664 | tf_op jit(solution)/shard_map/ppermute | solution.py:359
  2.3 10.3 %collective-permute-start = (bf16[128,1280]{1,0:T(8,128)(2,1)S(1)}, bf16[128,1280]{1,0:T(8,128)(2,1)S(1)}, u32[]{:S(2)}, u32[]{:S(2)}) collective-permute-start(bf16[128,1280]{1,0:T(8,128)(2,1)S(1)} %slice.82), channel_id=1, source_target_pairs={{0,64},{32,96},{64,0},{96,32},{1,65},{33,97},{65,1},{97,33},{2,66}... | collective-permute-start | bytes 983048 | tf_op jit(solution)/shard_map/ppermute | solution.py:356
  7.6 6.1 %copy-start.4 = (bf16[2,8,32,1280]{3,2,1,0:T(8,128)(2,1)S(1)}, bf16[2,8,32,1280]{3,2,1,0:T(8,128)(2,1)}, u32[]{:S(2)}) copy-start(bf16[2,8,32,1280]{3,2,1,0:T(8,128)(2,1)} %param.10) | copy-start | bytes 3932164
  7.6 11.9 %copy-start.5 = (bf16[1536,384]{1,0:T(8,128)(2,1)S(1)}, bf16[1536,384]{1,0:T(8,128)(2,1)}, u32[]{:S(2)}) copy-start(bf16[1536,384]{1,0:T(8,128)(2,1)} %refs_5_.1) | copy-start | bytes 3538948
  7.6 11.9 %copy-start.6 = (bf16[1280,320]{0,1:T(8,128)(2,1)S(1)}, bf16[1280,320]{0,1:T(8,128)(2,1)}, u32[]{:S(2)}) copy-start(bf16[1280,320]{0,1:T(8,128)(2,1)} %param.19) | copy-start | bytes 2457604
  7.6 11.9 %copy-start.10 = (bf16[1152,288]{0,1:T(8,128)(2,1)S(1)}, bf16[1152,288]{0,1:T(8,128)(2,1)}, u32[]{:S(2)}) copy-start(bf16[1152,288]{0,1:T(8,128)(2,1)} %param.17) | copy-start | bytes 1990660
  13.6 4.5 %collective-permute-start.5 = (bf16[1024,1152]{1,0:T(8,128)(2,1)S(1)}, bf16[1024,1152]{1,0:T(8,128)(2,1)S(1)}, u32[]{:S(2)}, u32[]{:S(2)}) collective-permute-start(bf16[1024,1152]{1,0:T(8,128)(2,1)S(1)} %bitcast.33), channel_id=1, source_target_pairs={{0,32},{32,0},{64,96},{96,64},{1,33},{33,1},{65,97},{97,65},{2,34}... | collective-permute-start | bytes 7077896 | tf_op jit(solution)/shard_map/ppermute | solution.py:364
  13.8 24.3 %collective-permute-start.4 = (bf16[384,1280]{1,0:T(8,128)(2,1)S(1)}, bf16[384,1280]{1,0:T(8,128)(2,1)S(1)}, u32[]{:S(2)}, u32[]{:S(2)}) collective-permute-start(bf16[384,1280]{1,0:T(8,128)(2,1)S(1)} %slice.83), channel_id=1, source_target_pairs={{0,64},{32,96},{64,0},{96,32},{1,65},{33,97},{65,1},{97,33},{2,66}... | collective-permute-start | bytes 2949128 | tf_op jit(solution)/shard_map/ppermute | solution.py:356
  20.7 17.4 %copy-start.1 = (bf16[2,2,256,1152]{3,2,1,0:T(8,128)(2,1)S(1)}, bf16[2,2,256,1152]{3,2,1,0:T(8,128)(2,1)}, u32[]{:S(2)}) copy-start(bf16[2,2,256,1152]{3,2,1,0:T(8,128)(2,1)} %copy-done) | copy-start | bytes 7077892
  39.7 9.4 %copy-start.9 = (bf16[320,1280]{1,0:T(8,128)(2,1)S(1)}, bf16[320,1280]{1,0:T(8,128)(2,1)}, u32[]{:S(2)}) copy-start(bf16[320,1280]{1,0:T(8,128)(2,1)} %copy-done.7) | copy-start | bytes 2457604
  39.7 9.4 %copy-start.11 = (bf16[1152,288]{0,1:T(8,128)(2,1)S(1)}, bf16[1152,288]{0,1:T(8,128)(2,1)}, u32[]{:S(2)}) copy-start(bf16[1152,288]{0,1:T(8,128)(2,1)} %param.17) | copy-start | bytes 1990660
  39.7 9.4 %copy-start.12 = (bf16[1024,1152]{1,0:T(8,128)(2,1)S(1)}, bf16[1024,1152]{1,0:T(8,128)(2,1)}, u32[]{:S(2)}) copy-start(bf16[1024,1152]{1,0:T(8,128)(2,1)} %get-tuple-element.62.refs_15_) | copy-start | bytes 7077892
  39.7 9.4 %copy-start.13 = (bf16[1024,768]{1,0:T(8,128)(2,1)S(1)}, bf16[1024,768]{1,0:T(8,128)(2,1)}, u32[]{:S(2)}) copy-start(bf16[1024,768]{1,0:T(8,128)(2,1)} %get-tuple-element.61.refs_14_) | copy-start | bytes 4718596
  47.6 15.1 %collective-permute-start.6 = (f32[8,1024]{1,0:T(8,128)S(1)}, f32[8,1024]{1,0:T(8,128)S(1)}, u32[]{:S(2)}, u32[]{:S(2)}) collective-permute-start(f32[8,1024]{1,0:T(8,128)S(1)} %get-tuple-element.54), channel_id=1, source_target_pairs={{0,64},{32,96},{64,0},{96,32},{1,65},{33,97},{65,1},{97,33},{2,66}... | collective-permute-start | bytes 98312 | tf_op jit(solution)/shard_map/ppermute | solution.py:380
  49.2 13.6 %copy-start.17 = (bf16[1024,1536]{1,0:T(8,128)(2,1)S(1)}, bf16[1024,1536]{1,0:T(8,128)(2,1)}, u32[]{:S(2)}) copy-start(bf16[1024,1536]{1,0:T(8,128)(2,1)} %get-tuple-element.53) | copy-start | bytes 9437188
  49.2 13.6 %copy-start.18 = (f32[1024,768]{1,0:T(8,128)S(1)}, f32[1024,768]{1,0:T(8,128)}, u32[]{:S(2)}) copy-start(f32[1024,768]{1,0:T(8,128)} %get-tuple-element.69) | copy-start | bytes 9437188
  60.6 5.6 %collective-permute-start.8 = (f32[8,1024]{1,0:T(8,128)S(1)}, f32[8,1024]{1,0:T(8,128)S(1)}, u32[]{:S(2)}, u32[]{:S(2)}) collective-permute-start(f32[8,1024]{1,0:T(8,128)S(1)} %get-tuple-element.65), channel_id=1, source_target_pairs={{0,64},{32,96},{64,0},{96,32},{1,65},{33,97},{65,1},{97,33},{2,66}... | collective-permute-start | bytes 98312 | tf_op jit(solution)/shard_map/ppermute | solution.py:380
  61.2 8.3 %collective-permute-start.10 = (f32[8,1024]{1,0:T(8,128)S(1)}, f32[8,1024]{1,0:T(8,128)S(1)}, u32[]{:S(2)}, u32[]{:S(2)}) collective-permute-start(f32[8,1024]{1,0:T(8,128)S(1)} %get-tuple-element.76), channel_id=1, source_target_pairs={{0,64},{32,96},{64,0},{96,32},{1,65},{33,97},{65,1},{97,33},{2,66}... | collective-permute-start | bytes 98312 | tf_op jit(solution)/shard_map/ppermute | solution.py:380
  62.8 3.5 %copy-start.15 = (f32[1024,768]{1,0:T(8,128)S(1)}, f32[1024,768]{1,0:T(8,128)}, u32[]{:S(2)}) copy-start(f32[1024,768]{1,0:T(8,128)} %get-tuple-element.74) | copy-start | bytes 9437188
  65.8 8.7 %collective-permute-start.7 = (bf16[1536,384]{1,0:T(8,128)(2,1)S(1)}, bf16[1536,384]{1,0:T(8,128)(2,1)S(1)}, u32[]{:S(2)}, u32[]{:S(2)}) collective-permute-start(bf16[1536,384]{1,0:T(8,128)(2,1)S(1)} %slice.89), channel_id=1, source_target_pairs={{0,32},{32,0},{64,96},{96,64},{1,33},{33,1},{65,97},{97,65},{2,34}... | collective-permute-start | bytes 3538952 | tf_op jit(solution)/shard_map/ppermute | solution.py:397
  68.9 5.6 %collective-permute-start.9 = (bf16[1280,384]{1,0:T(8,128)(2,1)S(1)}, bf16[1280,384]{1,0:T(8,128)(2,1)S(1)}, u32[]{:S(2)}, u32[]{:S(2)}) collective-permute-start(bf16[1280,384]{1,0:T(8,128)(2,1)S(1)} %slice.95), channel_id=1, source_target_pairs={{0,32},{32,0},{64,96},{96,64},{1,33},{33,1},{65,97},{97,65},{2,34}... | collective-permute-start | bytes 2949128 | tf_op jit(solution)/shard_map/ppermute | solution.py:397
  72.0 2.5 %collective-permute-start.11 = (bf16[1152,384]{1,0:T(8,128)(2,1)S(1)}, bf16[1152,384]{1,0:T(8,128)(2,1)S(1)}, u32[]{:S(2)}, u32[]{:S(2)}) collective-permute-start(bf16[1152,384]{1,0:T(8,128)(2,1)S(1)} %slice.101), channel_id=1, source_target_pairs={{0,32},{32,0},{64,96},{96,64},{1,33},{33,1},{65,97},{97,65},{2,34}... | collective-permute-start | bytes 2654216 | tf_op jit(solution)/shard_map/ppermute | solution.py:397
  (9 other events, 16.9 us)

commit v3 on v2

--- a/solution.py
+++ b/solution.py
@@ -117,11 +117,11 @@
 def adapt_kernel(which, fresh, turned, slots, pieces, *refs):
     teachers = len(turned)
     x_in, refs = copies_of(refs, pieces)
-    (goal_o_in, goal_s_in), refs = copies_of(refs, 2)
+    goals_in, refs = copies_of(refs, 2 if fresh else teachers)
     ins, refs = copies_of(refs, 3 * teachers)
     if not fresh:
-        refs = refs[4 * teachers :]
-    outs, refs = copies_of(refs, 4 * teachers)
+        refs = refs[3 * teachers :]
+    outs, refs = copies_of(refs, (4 if fresh else 3) * teachers)
     x, refs = refs[0], refs[1:]
     bufs, refs = copies_of(refs, 6 * teachers)
     in_sem, w1_sem, out_sem = refs
@@ -159,9 +159,14 @@
         pairs = (
             (w2o_in, w2o),
             (w2s_in, w2s),
-            (goal_o_in.at[at_out, lanes], goal.at[:, pl.ds(0, HALF)]),
-            (goal_s_in.at[at_out, lanes], goal.at[:, pl.ds(HALF, HALF)]),
         )
+        if fresh:
+            pairs += tuple(
+                (side.at[at_out, lanes], goal.at[:, pl.ds(i * HALF, HALF)])
+                for i, side in enumerate(goals_in)
+            )
+        else:
+            pairs += ((goals_in[t].at[at_out], goal),)
         group = [
             pltpu.make_async_copy(src, dst, in_sem.at[5 * t + i])
             for i, (src, dst) in enumerate(pairs)
@@ -177,10 +182,23 @@
     for copy in tokens:
         copy.wait()
     stores = []
+    if fresh:
+        later = pl.ds(rows, rows)
+        for t in range(teachers):
+            for i, side in enumerate(goals_in):
+                copy = pltpu.make_async_copy(
+                    side.at[later, pl.ds(slots[t] * HALF, HALF)],
+                    outs[4 * t].at[later, pl.ds(i * HALF, HALF)],
+                    out_sem.at[4 * teachers + 2 * t + i],
+                )
+                copy.start()
+                stores.append(copy)
 
     def send(t, i):
         copy_from = bufs[6 * t + 2 + i]
-        target = outs[4 * t + i]
+        if i == 0 and not fresh:
+            return
+        target = outs[4 * t + i if fresh else 3 * t + i - 1]
         target = target.at[:, at_out] if i == 3 else target.at[at_out]
         copy = pltpu.make_async_copy(copy_from, target, out_sem.at[4 * t + i])
         copy.start()
@@ -229,8 +247,9 @@
     for (w1, *_), turn in zip(teachers, turned):
         channels = w1.shape[1]
         wide = 2 * HALF
+        if prior is None:
+            outs.append(jax.ShapeDtypeStruct((2 * rows, wide), bf16))
         outs += [
-            jax.ShapeDtypeStruct((2 * rows, wide), bf16),
             jax.ShapeDtypeStruct((2 * rows, channels), bf16),
             jax.ShapeDtypeStruct((2 * rows, wide), f32),
             jax.ShapeDtypeStruct((8, 2 * rows), f32),
@@ -247,7 +266,7 @@
     scratch += [
         pltpu.SemaphoreType.DMA((5 * n + len(pieces),)),
         pltpu.SemaphoreType.DMA((4 * n,)),
-        pltpu.SemaphoreType.DMA((4 * n,)),
+        pltpu.SemaphoreType.DMA((6 * n,)),
     ]
     args = [*pieces, *goals] + [a for teacher in teachers for a in teacher]
     aliases = {}
@@ -371,7 +390,11 @@
         if after is not None:
             *pieces, after = lax.optimization_barrier((*pieces, after))
         slots = tuple(range(i, to))
-        return adapt(pieces, 1, goals, teachers[i:to], slots, firsts[4 * i : 4 * to])
+        held = [firsts[4 * t : 4 * t + 4] for t in slots]
+        results = adapt(
+            pieces, 1, [h[0] for h in held], teachers[i:to], slots, [r for h in held for r in h[1:]]
+        )
+        return [r for k, h in enumerate(held) for r in (h[0], *results[3 * k : 3 * k + 3])]
 
     def gradient(state, after):
         goal, hidden, pred, part = state

time: 125 us -> 137 us (1.096)
  Pallas kernels: 40.6 us -> 51.8 us
  waiting for transfers between devices: 7.4 us -> 5.08 us
  matrix products: 7.71 us -> 9.98 us
    pallas_call x3, Pallas kernels: 34.3 us -> 45.6 us  [adapt(): pl.pallas_call(functools.partial(adapt_kernel, which, prior is None, turn...]
    ppermute x2, waiting for transfers between devices: 2.29 us -> 0.01 us  [shards(): lax.ppermute(piece, 'grp', CHIP)]
    dot_general x3, matrix products: 7.71 us -> 9.98 us  [gradient(): grad = jnp.einsum('tk,tc->kc', hidden, error, preferred_element_type=f32)]
    unnamed x44 -> x34, local copies, waits for them, and re-layouts: 10.1 us -> 11.3 us
  transfers between devices with their start and end apart: 12 -> 12, of which waited for: 3 -> 2; matrix products, arithmetic and copies ran while one was open for 9% -> 10% of each run, Pallas kernels for 24% -> 30%
where the time goes in v3:
time: 137 us
  Pallas kernels  51.8 us (38%)
  blocking collectives  47.4 us (35%)
  local copies, waits for them, and re-layouts  12.7 us (9%)
  matrix products  9.98 us (7%)
  starting transfers between devices  8.92 us (7%)
  waiting for transfers between devices  5.08 us (4%)
    all_to_all x1, blocking collectives, shards(): split = lax.all_to_all(pack(grads, received, n_dp), 'dp', 0, 0, tiled=True)  47.4 us
    pallas_call x3, Pallas kernels, adapt(): pl.pallas_call(functools.partial(adapt_kernel, which, prior is None, turn...  45.6 us
    unnamed x34, local copies, waits for them, and re-layouts  11.3 us
    dot_general x3, matrix products, gradient(): grad = jnp.einsum('tk,tc->kc', hidden, error, preferred_element_type=f32)  9.98 us
    ppermute x3, starting transfers between devices, gradient(): sums = part + jnp.roll(lax.ppermute(part, 'grp', CHIP), own_tokens, axis=1)  3.62 us
    pallas_call x1, Pallas kernels, targets(): pl.pallas_call(targets_kernel, grid_spec=pltpu.PrefetchScalarGridSpec(num...  3.56 us
    ppermute x2, starting transfers between devices, shards(): lax.ppermute(piece, 'grp', CHIP)  3.39 us
  transfers between devices with their start and end apart: 12, of which 2 were waited for; matrix products, arithmetic and copies ran while one was open for 10% of the time, Pallas kernels for 30%

profile of v3, /device:TPU:0, one launch (start us, length us, event | category | flops | bytes accessed | tf_op | source)
XLA Modules:
  0.0 137.0 jit_solution(2582874268253029201)
XLA Ops:
  1.3 1.0 slice.82
  2.3 1.7 %collective-permute-start = (bf16[128,1280]{1,0:T(8,128)(2,1)S(1)}, bf16[128,1280]{1,0:T(8,128)(2,1)S(1)}, u32[]{:S(2)}, u32[]{:S(2)}) collective-permute-start(bf16[128,1280]{1,0:T(8,128)(2,1)S(1)} %slice.82), channel_id=1, source_target_pairs={{0,64},{32,96},{64,0},{96,32},{1,65},{33,97},{65,1},{97,33},{2,66}... | collective-permute-start | bytes 983048 | tf_op jit(solution)/shard_map/ppermute | solution.py:375
  4.1 2.0 %copy.22.dino = bf16[2,36,36,384]{3,2,1,0:T(8,128)(2,1)S(1)} copy(bf16[2,36,36,384]{3,0,2,1:T(2,128)(2,1)} %param.11) | data formatting | bytes 3981312 | tf_op args[1]
  6.6 1.0 copy-done.9
  7.6 3.6 %targets.1 = (bf16[2,2,256,1152]{3,2,1,0:T(8,128)(2,1)S(1)}, bf16[2,2,256,1152]{3,2,1,0:T(8,128)(2,1)S(1)}) custom-call(s32[4]{0:T(128)S(1)} %pad_add_fusion.order_ref, bf16[2,36,36,384]{3,2,1,0:T(8,128)(2,1)S(1)} %copy.22.dino, bf16[2,36,36,288]{3,2,1,0:T(8,128)(2,1)S(1)} %copy.23.siglip, bf16[2,32,32,320]{3,2,1,0:T(8,128)(2,1)S(1)} %copy-done.9), custom_call_target="tpu_custom_call" | custom-call | flops 1000 | bytes 1000 | tf_op jit(solution)/shard_map/targets/pallas_call | solution.py:87
  11.2 1.4 %copy-done.7 = bf16[2,2,256,1152]{3,2,1,0:T(8,128)(2,1)} copy-done((bf16[2,2,256,1152]{3,2,1,0:T(8,128)(2,1)}, bf16[2,2,256,1152]{3,2,1,0:T(8,128)(2,1)S(1)}, u32[]{:S(2)}) %copy-start.7) | copy-done | bytes 2359320
  12.9 1.6 %collective-permute-start.4 = (bf16[384,1280]{1,0:T(8,128)(2,1)S(1)}, bf16[384,1280]{1,0:T(8,128)(2,1)S(1)}, u32[]{:S(2)}, u32[]{:S(2)}) collective-permute-start(bf16[384,1280]{1,0:T(8,128)(2,1)S(1)} %slice.83), channel_id=1, source_target_pairs={{0,64},{32,96},{64,0},{96,32},{1,65},{33,97},{65,1},{97,33},{2,66}... | collective-permute-start | bytes 2949128 | tf_op jit(solution)/shard_map/ppermute | solution.py:375
  14.5 2.7 %collective-permute-done.5.refs_2_ = bf16[1024,1152]{1,0:T(8,128)(2,1)S(1)} collective-permute-done((bf16[1024,1152]{1,0:T(8,128)(2,1)S(1)}, bf16[1024,1152]{1,0:T(8,128)(2,1)S(1)}, u32[]{:S(2)}, u32[]{:S(2)}) %collective-permute-start.5) | collective-permute-done | bytes 2359328 | tf_op jit(solution)/shard_map/ppermute | solution.py:383
  17.2 1.4 %copy-done.14 = bf16[1024,1152]{1,0:T(8,128)(2,1)} copy-done((bf16[1024,1152]{1,0:T(8,128)(2,1)}, bf16[1024,1152]{1,0:T(8,128)(2,1)S(1)}, u32[]{:S(2)}) %copy-start.14) | copy-done | bytes 2359320
  18.6 26.4 %adapt.3 = (bf16[1024,768]{1,0:T(8,128)(2,1)S(1)}, bf16[1024,1536]{1,0:T(8,128)(2,1)}, f32[1024,768]{1,0:T(8,128)}, f32[8,1024]{1,0:T(8,128)S(1)}, bf16[1024,768...) custom-call(bf16[512,1280]{1,0:T(8,128)(2,1)S(1)} %bitcast.23, ...), custom_call_target="tpu_custom_call" | custom-call | flops 1000 | bytes 1000 | tf_op jit(solution)/shard_map/adapt/pallas_call | solution.py:277
  45.1 1.9 %copy-done.3 = bf16[1024,1536]{1,0:T(8,128)(2,1)S(1)} copy-done((bf16[1024,1536]{1,0:T(8,128)(2,1)S(1)}, bf16[1024,1536]{1,0:T(8,128)(2,1)}, u32[]{:S(2)}) %copy-start.3) | copy-done | bytes 3145752
  46.9 7.9 %adapt.4 = (bf16[1024,1536]{1,0:T(8,128)(2,1)S(1)}, f32[1024,768]{1,0:T(8,128)}, f32[8,1024]{1,0:T(8,128)S(1)}) custom-call(bf16[128,1280]{1,0:T(8,128)(2,1)S(1)} %collective-permute-done.refs_0_, bf16[384,1280]{1,0:T(8,128)(2,1)S(1)} %collective-permute-done.4.refs_1_, ...), custom_call_target="tpu_custom_call", output_to_operand_aliasing={{0}: (6, {}), {1}: (7, {}), {2}: (8, {})} | custom-call | flops 1000 | bytes 1000 | tf_op jit(solution)/shard_map/adapt/pallas_call | solution.py:277
  54.8 1.7 %copy-done.4 = bf16[1024,1536]{1,0:T(8,128)(2,1)} copy-done((bf16[1024,1536]{1,0:T(8,128)(2,1)}, bf16[1024,1536]{1,0:T(8,128)(2,1)S(1)}, u32[]{:S(2)}) %copy-start.4) | copy-done | bytes 3145752
  56.5 1.5 %collective-permute-start.6 = (f32[8,1024]{1,0:T(8,128)S(1)}, f32[8,1024]{1,0:T(8,128)S(1)}, u32[]{:S(2)}, u32[]{:S(2)}) collective-permute-start(f32[8,1024]{1,0:T(8,128)S(1)} %get-tuple-element.51), channel_id=1, source_target_pairs={{0,64},{32,96},{64,0},{96,32},{1,65},{33,97},{65,1},{97,33},{2,66}... | collective-permute-start | bytes 98312 | tf_op jit(solution)/shard_map/ppermute | solution.py:403
  58.0 1.4 %copy-done.10 = bf16[1024,768]{1,0:T(8,128)(2,1)S(1)} copy-done((bf16[1024,768]{1,0:T(8,128)(2,1)S(1)}, bf16[1024,768]{1,0:T(8,128)(2,1)}, u32[]{:S(2)}) %copy-start.10) | copy-done | bytes 1572888
  59.5 11.3 %adapt.5 = (bf16[1024,1280]{1,0:T(8,128)(2,1)}, f32[1024,768]{1,0:T(8,128)}, f32[8,1024]{1,0:T(8,128)S(1)}, bf16[1024,1152]{1,0:T(8,128)(2,1)S(1)}, f32[1024,768]{1,0:T(8,128)}, /*index=5*/f32[8,1024]{1,0:T(8,128)S(1)}) custom-call(bf16[128,1280]{1,0:T(8,128)(2,1)S(1)} %collective-permut, ...), custom_call_target="tpu_custom_call", output_to_operand_aliasing={{0}: (10, {}), {1}: (11, {}), {2}: (12, {}), {3}: (13, {}),... | custom-call | flops 1000 | bytes 1000 | tf_op jit(solution)/shard_map/adapt/pallas_call | solution.py:277
  71.4 1.5 %collective-permute-start.10 = (f32[8,1024]{1,0:T(8,128)S(1)}, f32[8,1024]{1,0:T(8,128)S(1)}, u32[]{:S(2)}, u32[]{:S(2)}) collective-permute-start(f32[8,1024]{1,0:T(8,128)S(1)} %get-tuple-element.71), channel_id=1, source_target_pairs={{0,64},{32,96},{64,0},{96,32},{1,65},{33,97},{65,1},{97,33},{2,66}... | collective-permute-start | bytes 98312 | tf_op jit(solution)/shard_map/ppermute | solution.py:403
  73.0 5.0 %convolution_convert_fusion.dino = bf16[1536,768]{1,0:T(8,128)(2,1)S(1)} fusion(bf16[1024,1536]{1,0:T(8,128)(2,1)S(1)} %copy-done.5, f32[1024,768]{1,0:T(8,128)} %get-tuple-element.65, bf16[1024,768]{1,0:T(8,128)(2,1)S(1)} %get-tuple-element.46.refs_2_, f32[1024]{0:T(1024)S(1)} %get-tuple-element.64, f32[1024]{0:T(1024)S(1)} %get-tuple-element.63), kind=kOutput, calls=%fused_computation | convolution fusion | flops 2421030912 | bytes 10231808 | tf_op jit(solution)/shard_map/tk,tc->kc/dot_general | solution.py:411
  78.6 2.6 %convolution_convert_fusion.2.sam = bf16[1280,768]{1,0:T(8,128)(2,1)S(1)} fusion(bf16[1024,1280]{1,0:T(8,128)(2,1)S(1)} %copy-done.13, f32[1024,768]{1,0:T(8,128)S(1)} %copy-done.11, bf16[1024,768]{1,0:T(8,128)(2,1)S(1)} %get-tuple-element.54.refs_2_, f32[1024]{0:T(1024)S(1)} %get-tuple-element.68, f32[1024]{0:T(1024)S(1)} %get-tuple-element.67), kind=kOutput, calls=%fused_computation.2 | convolution fusion | flops 2018181120 | bytes 9314304 | tf_op jit(solution)/shard_map/tk,tc->kc/dot_general | solution.py:411
  82.0 2.3 %convolution_convert_fusion.1.siglip = bf16[1152,768]{1,0:T(8,128)(2,1)S(1)} fusion(bf16[1024,1152]{1,0:T(8,128)(2,1)S(1)} %get-tuple-element.70, f32[1024,768]{1,0:T(8,128)S(1)} %copy-done.12, bf16[1024,768]{1,0:T(8,128)(2,1)S(1)} %copy-done.10, f32[1024]{0:T(1024)S(1)} %get-tuple-element.73, f32[1024]{0:T(1024)S(1)} %get-tuple-element.72), kind=kOutput, calls=%fused_computation.1 | convolution fusion | flops 1816756224 | bytes 8855552 | tf_op jit(solution)/shard_map/tk,tc->kc/dot_general | solution.py:411
  84.5 2.4 %collective-permute-done.11.siglip_other = bf16[1152,384]{1,0:T(8,128)(2,1)S(1)} collective-permute-done((bf16[1152,384]{1,0:T(8,128)(2,1)S(1)}, bf16[1152,384]{1,0:T(8,128)(2,1)S(1)}, u32[]{:S(2)}, u32[]{:S(2)}) %collective-permute-start.11) | collective-permute-done | bytes 884768 | tf_op jit(solution)/shard_map/ppermute | solution.py:420
  86.9 1.6 %pack.1 = bf16[32,336,128]{2,1,0:T(8,128)(2,1)S(1)} custom-call(bf16[1536,768]{1,0:T(8,128)(2,1)S(1)} %convolution_convert_fusion.dino, bf16[1536,384]{1,0:T(8,128)(2,1)S(1)} %collective-permute-done.7.dino_other, bf16[1280,768]{1,0:T(8,128)(2,1)S(1)} %convolution_convert_fusion.2.sam, bf16[1280,384]{1,0:T(8,128)(2,1)S(1)} %collective-permute-done.9.sam_other, ...), custom_call_target="tpu_custom_call" | custom-call | tf_op jit(solution)/shard_map/pack/pallas_call | solution.py:315
  88.6 47.4 %all_to_all.5.split = bf16[32,336,128]{2,1,0:T(8,128)(2,1)S(1)} all-to-all(bf16[32,336,128]{2,1,0:T(8,128)(2,1)S(1)} %pack.1), channel_id=1, replica_groups=mesh['grp'=4,'dp'=32] {'dp'}, dimensions={0} | all-to-all | bytes 5505024 | tf_op jit(solution)/shard_map/all_to_all | solution.py:421
  136.0 1.1 unpack.1
  (62 shorter events, 3.7 us)
Async XLA Ops:
  0.6 12.0 %collective-permute-start.1 = (bf16[1536,384]{1,0:T(8,128)(2,1)}, bf16[1536,384]{1,0:T(8,128)(2,1)S(1)}, u32[]{:S(2)}, u32[]{:S(2)}) collective-permute-start(bf16[1536,384]{1,0:T(8,128)(2,1)} %refs_4_.4), channel_id=1, source_target_pairs={{0,32},{32,0},{64,96},{96,64},{1,33},{33,1},{65,97},{97,65},{2,34}... | collective-permute-start | bytes 3538952 | tf_op jit(solution)/shard_map/ppermute | solution.py:378
  0.7 11.9 %collective-permute-start.2 = (bf16[320,1280]{1,0:T(8,128)(2,1)}, bf16[320,1280]{1,0:T(8,128)(2,1)S(1)}, u32[]{:S(2)}, u32[]{:S(2)}) collective-permute-start(bf16[320,1280]{1,0:T(8,128)(2,1)} %bitcast.24), channel_id=1, source_target_pairs={{0,32},{32,0},{64,96},{96,64},{1,33},{33,1},{65,97},{97,65},{2,34}... | collective-permute-start | bytes 2457608 | tf_op jit(solution)/shard_map/ppermute | solution.py:378
  1.2 11.4 %collective-permute-start.3 = (bf16[288,1152]{1,0:T(8,128)(2,1)}, bf16[288,1152]{1,0:T(8,128)(2,1)S(1)}, u32[]{:S(2)}, u32[]{:S(2)}) collective-permute-start(bf16[288,1152]{1,0:T(8,128)(2,1)} %bitcast.27), channel_id=1, source_target_pairs={{0,32},{32,0},{64,96},{96,64},{1,33},{33,1},{65,97},{97,65},{2,34}... | collective-permute-start | bytes 1990664 | tf_op jit(solution)/shard_map/ppermute | solution.py:378
  2.3 10.3 %collective-permute-start = (bf16[128,1280]{1,0:T(8,128)(2,1)S(1)}, bf16[128,1280]{1,0:T(8,128)(2,1)S(1)}, u32[]{:S(2)}, u32[]{:S(2)}) collective-permute-start(bf16[128,1280]{1,0:T(8,128)(2,1)S(1)} %slice.82), channel_id=1, source_target_pairs={{0,64},{32,96},{64,0},{96,32},{1,65},{33,97},{65,1},{97,33},{2,66}... | collective-permute-start | bytes 983048 | tf_op jit(solution)/shard_map/ppermute | solution.py:375
  4.1 2.2 %copy-start.15 = (bf16[2,36,36,288]{3,0,2,1:T(2,128)(2,1)S(1)}, bf16[2,36,36,288]{3,0,2,1:T(2,128)(2,1)}, u32[]{:S(2)}) copy-start(bf16[2,36,36,288]{3,0,2,1:T(2,128)(2,1)} %param.12) | copy-start | bytes 4478980
  7.6 5.2 %copy-start = (bf16[2,8,32,1280]{3,2,1,0:T(8,128)(2,1)S(1)}, bf16[2,8,32,1280]{3,2,1,0:T(8,128)(2,1)}, u32[]{:S(2)}) copy-start(bf16[2,8,32,1280]{3,2,1,0:T(8,128)(2,1)} %param.10) | copy-start | bytes 3932164
  7.6 11.0 %copy-start.1 = (bf16[1536,384]{1,0:T(8,128)(2,1)S(1)}, bf16[1536,384]{1,0:T(8,128)(2,1)}, u32[]{:S(2)}) copy-start(bf16[1536,384]{1,0:T(8,128)(2,1)} %refs_4_.4) | copy-start | bytes 3538948
  7.6 11.0 %copy-start.2 = (bf16[1280,320]{0,1:T(8,128)(2,1)S(1)}, bf16[1280,320]{0,1:T(8,128)(2,1)}, u32[]{:S(2)}) copy-start(bf16[1280,320]{0,1:T(8,128)(2,1)} %param.19) | copy-start | bytes 2457604
  7.6 11.0 %copy-start.6 = (bf16[1152,288]{0,1:T(8,128)(2,1)S(1)}, bf16[1152,288]{0,1:T(8,128)(2,1)}, u32[]{:S(2)}) copy-start(bf16[1152,288]{0,1:T(8,128)(2,1)} %param.17) | copy-start | bytes 1990660
  12.6 4.6 %collective-permute-start.5 = (bf16[1024,1152]{1,0:T(8,128)(2,1)S(1)}, bf16[1024,1152]{1,0:T(8,128)(2,1)S(1)}, u32[]{:S(2)}, u32[]{:S(2)}) collective-permute-start(bf16[1024,1152]{1,0:T(8,128)(2,1)S(1)} %bitcast.31), channel_id=1, source_target_pairs={{0,32},{32,0},{64,96},{96,64},{1,33},{33,1},{65,97},{97,65},{2,34}... | collective-permute-start | bytes 7077896 | tf_op jit(solution)/shard_map/ppermute | solution.py:383
  12.9 32.1 %collective-permute-start.4 = (bf16[384,1280]{1,0:T(8,128)(2,1)S(1)}, bf16[384,1280]{1,0:T(8,128)(2,1)S(1)}, u32[]{:S(2)}, u32[]{:S(2)}) collective-permute-start(bf16[384,1280]{1,0:T(8,128)(2,1)S(1)} %slice.83), channel_id=1, source_target_pairs={{0,64},{32,96},{64,0},{96,32},{1,65},{33,97},{65,1},{97,33},{2,66}... | collective-permute-start | bytes 2949128 | tf_op jit(solution)/shard_map/ppermute | solution.py:375
  45.0 1.9 %copy-start.3 = (bf16[1024,1536]{1,0:T(8,128)(2,1)S(1)}, bf16[1024,1536]{1,0:T(8,128)(2,1)}, u32[]{:S(2)}) copy-start(bf16[1024,1536]{1,0:T(8,128)(2,1)} %get-tuple-element.47.refs_6_) | copy-start | bytes 9437188
  46.9 11.1 %copy-start.8 = (bf16[1024,1152]{1,0:T(8,128)(2,1)S(1)}, bf16[1024,1152]{1,0:T(8,128)(2,1)}, u32[]{:S(2)}) copy-start(bf16[1024,1152]{1,0:T(8,128)(2,1)} %get-tuple-element.59.refs_13_) | copy-start | bytes 7077892
  54.8 1.7 %copy-start.4 = (bf16[1024,1536]{1,0:T(8,128)(2,1)}, bf16[1024,1536]{1,0:T(8,128)(2,1)S(1)}, u32[]{:S(2)}) copy-start(bf16[1024,1536]{1,0:T(8,128)(2,1)S(1)} %get-tuple-element.50) | copy-start | bytes 9437188
  56.5 16.3 %collective-permute-start.6 = (f32[8,1024]{1,0:T(8,128)S(1)}, f32[8,1024]{1,0:T(8,128)S(1)}, u32[]{:S(2)}, u32[]{:S(2)}) collective-permute-start(f32[8,1024]{1,0:T(8,128)S(1)} %get-tuple-element.51), channel_id=1, source_target_pairs={{0,64},{32,96},{64,0},{96,32},{1,65},{33,97},{65,1},{97,33},{2,66}... | collective-permute-start | bytes 98312 | tf_op jit(solution)/shard_map/ppermute | solution.py:403
  59.4 13.5 %copy-start.5 = (bf16[1024,1536]{1,0:T(8,128)(2,1)S(1)}, bf16[1024,1536]{1,0:T(8,128)(2,1)}, u32[]{:S(2)}) copy-start(bf16[1024,1536]{1,0:T(8,128)(2,1)} %copy-done.4) | copy-start | bytes 9437188
  70.8 7.7 %collective-permute-start.8 = (f32[8,1024]{1,0:T(8,128)S(1)}, f32[8,1024]{1,0:T(8,128)S(1)}, u32[]{:S(2)}, u32[]{:S(2)}) collective-permute-start(f32[8,1024]{1,0:T(8,128)S(1)} %get-tuple-element.62), channel_id=1, source_target_pairs={{0,64},{32,96},{64,0},{96,32},{1,65},{33,97},{65,1},{97,33},{2,66}... | collective-permute-start | bytes 98312 | tf_op jit(solution)/shard_map/ppermute | solution.py:403
  71.4 10.6 %collective-permute-start.10 = (f32[8,1024]{1,0:T(8,128)S(1)}, f32[8,1024]{1,0:T(8,128)S(1)}, u32[]{:S(2)}, u32[]{:S(2)}) collective-permute-start(f32[8,1024]{1,0:T(8,128)S(1)} %get-tuple-element.71), channel_id=1, source_target_pairs={{0,64},{32,96},{64,0},{96,32},{1,65},{33,97},{65,1},{97,33},{2,66}... | collective-permute-start | bytes 98312 | tf_op jit(solution)/shard_map/ppermute | solution.py:403
  72.9 5.6 %copy-start.11 = (f32[1024,768]{1,0:T(8,128)S(1)}, f32[1024,768]{1,0:T(8,128)}, u32[]{:S(2)}) copy-start(f32[1024,768]{1,0:T(8,128)} %get-tuple-element.69) | copy-start | bytes 9437188
  73.0 5.6 %copy-start.13 = (bf16[1024,1280]{1,0:T(8,128)(2,1)S(1)}, bf16[1024,1280]{1,0:T(8,128)(2,1)}, u32[]{:S(2)}) copy-start(bf16[1024,1280]{1,0:T(8,128)(2,1)} %get-tuple-element.66) | copy-start | bytes 7864324
  78.1 8.8 %collective-permute-start.7 = (bf16[1536,384]{1,0:T(8,128)(2,1)S(1)}, bf16[1536,384]{1,0:T(8,128)(2,1)S(1)}, u32[]{:S(2)}, u32[]{:S(2)}) collective-permute-start(bf16[1536,384]{1,0:T(8,128)(2,1)S(1)} %slice.89), channel_id=1, source_target_pairs={{0,32},{32,0},{64,96},{96,64},{1,33},{33,1},{65,97},{97,65},{2,34}... | collective-permute-start | bytes 3538952 | tf_op jit(solution)/shard_map/ppermute | solution.py:420
  78.6 3.4 %copy-start.12 = (f32[1024,768]{1,0:T(8,128)S(1)}, f32[1024,768]{1,0:T(8,128)}, u32[]{:S(2)}) copy-start(f32[1024,768]{1,0:T(8,128)} %get-tuple-element.74) | copy-start | bytes 9437188
  81.4 5.6 %collective-permute-start.9 = (bf16[1280,384]{1,0:T(8,128)(2,1)S(1)}, bf16[1280,384]{1,0:T(8,128)(2,1)S(1)}, u32[]{:S(2)}, u32[]{:S(2)}) collective-permute-start(bf16[1280,384]{1,0:T(8,128)(2,1)S(1)} %slice.95), channel_id=1, source_target_pairs={{0,32},{32,0},{64,96},{96,64},{1,33},{33,1},{65,97},{97,65},{2,34}... | collective-permute-start | bytes 2949128 | tf_op jit(solution)/shard_map/ppermute | solution.py:420
  84.4 2.5 %collective-permute-start.11 = (bf16[1152,384]{1,0:T(8,128)(2,1)S(1)}, bf16[1152,384]{1,0:T(8,128)(2,1)S(1)}, u32[]{:S(2)}, u32[]{:S(2)}) collective-permute-start(bf16[1152,384]{1,0:T(8,128)(2,1)S(1)} %slice.101), channel_id=1, source_target_pairs={{0,32},{32,0},{64,96},{96,64},{1,33},{33,1},{65,97},{97,65},{2,34}... | collective-permute-start | bytes 2654216 | tf_op jit(solution)/shard_map/ppermute | solution.py:420
  (4 other events, 5.6 us)

commit v4 on v2

--- a/solution.py
+++ b/solution.py
@@ -262,7 +262,7 @@
         out_shape=outs,
         scratch_shapes=scratch,
         input_output_aliases=aliases,
-        compiler_params=pltpu.CompilerParams(vmem_limit_bytes=44 * MIB),
+        compiler_params=pltpu.CompilerParams(vmem_limit_bytes={1: 61, 2: 50, 3: 44}[n] * MIB),
         cost_estimate=pl.CostEstimate(flops=1000, bytes_accessed=1000, transcendentals=0),
         name="adapt",
     )(*args)

time: 125 us -> 123 us (0.984)
  waiting for transfers between devices: 7.4 us -> 4.91 us
    ppermute x2, waiting for transfers between devices: 2.29 us -> 0.01 us  [shards(): lax.ppermute(piece, 'grp', CHIP)]
    unnamed x44 -> x58, local copies, waits for them, and re-layouts: 10.1 us -> 10.9 us
  transfers between devices with their start and end apart: 12 -> 12, of which waited for: 3 -> 2; matrix products, arithmetic and copies ran while one was open for 9% -> 9% of each run, Pallas kernels for 24% -> 24%
where the time goes in v4:
time: 123 us
  blocking collectives  47.4 us (39%)
  Pallas kernels  40.3 us (33%)
  local copies, waits for them, and re-layouts  12.3 us (10%)
  starting transfers between devices  8.89 us (7%)
  matrix products  7.72 us (6%)
  waiting for transfers between devices  4.91 us (4%)
    all_to_all x1, blocking collectives, shards(): split = lax.all_to_all(pack(grads, received, n_dp), 'dp', 0, 0, tiled=True)  47.4 us
    pallas_call x3, Pallas kernels, adapt(): pl.pallas_call(functools.partial(adapt_kernel, which, prior is None, turn...  34 us
    unnamed x58, local copies, waits for them, and re-layouts  10.9 us
    dot_general x3, matrix products, gradient(): grad = jnp.einsum('tk,tc->kc', hidden, error, preferred_element_type=f32)  7.72 us
    ppermute x3, starting transfers between devices, gradient(): sums = part + jnp.roll(lax.ppermute(part, 'grp', CHIP), own_tokens, axis=1)  3.67 us
    pallas_call x1, Pallas kernels, targets(): pl.pallas_call(targets_kernel, grid_spec=pltpu.PrefetchScalarGridSpec(num...  3.56 us
    ppermute x2, starting transfers between devices, shards(): lax.ppermute(piece, 'grp', CHIP)  3.37 us
    ppermute x1, waiting for transfers between devices, shards(): goals = (kept, lax.ppermute(sent, 'grp', CORE))  2.69 us
  transfers between devices with their start and end apart: 12, of which 2 were waited for; matrix products, arithmetic and copies ran while one was open for 9% of the time, Pallas kernels for 24%

profile of v4, /device:TPU:0, one launch (start us, length us, event | category | flops | bytes accessed | tf_op | source)
XLA Modules:
  0.0 122.8 jit_solution(9443597265319448692)
XLA Ops:
  1.3 1.0 slice.82
  2.3 1.7 %collective-permute-start = (bf16[128,1280]{1,0:T(8,128)(2,1)S(1)}, bf16[128,1280]{1,0:T(8,128)(2,1)S(1)}, u32[]{:S(2)}, u32[]{:S(2)}) collective-permute-start(bf16[128,1280]{1,0:T(8,128)(2,1)S(1)} %slice.82), channel_id=1, source_target_pairs={{0,64},{32,96},{64,0},{96,32},{1,65},{33,97},{65,1},{97,33},{2,66}... | collective-permute-start | bytes 983048 | tf_op jit(solution)/shard_map/ppermute | solution.py:356
  4.1 2.0 %copy.25.dino = bf16[2,36,36,384]{3,2,1,0:T(8,128)(2,1)S(1)} copy(bf16[2,36,36,384]{3,0,2,1:T(2,128)(2,1)} %param.11) | data formatting | bytes 3981312 | tf_op args[1]
  6.6 1.0 copy-done.11
  7.6 3.6 %targets.1 = (bf16[2,2,256,1152]{3,2,1,0:T(8,128)(2,1)S(1)}, bf16[2,2,256,1152]{3,2,1,0:T(8,128)(2,1)S(1)}) custom-call(s32[4]{0:T(128)S(1)} %pad_add_fusion.order_ref, bf16[2,36,36,384]{3,2,1,0:T(8,128)(2,1)S(1)} %copy.25.dino, bf16[2,36,36,288]{3,2,1,0:T(8,128)(2,1)S(1)} %copy.26.siglip, bf16[2,32,32,320]{3,2,1,0:T(8,128)(2,1)S(1)} %copy-done.11), custom_call_target="tpu_custom_call" | custom-call | flops 1000 | bytes 1000 | tf_op jit(solution)/shard_map/targets/pallas_call | solution.py:87
  11.2 1.4 %copy-done = bf16[2,2,256,1152]{3,2,1,0:T(8,128)(2,1)} copy-done((bf16[2,2,256,1152]{3,2,1,0:T(8,128)(2,1)}, bf16[2,2,256,1152]{3,2,1,0:T(8,128)(2,1)S(1)}, u32[]{:S(2)}) %copy-start) | copy-done | bytes 2359320
  12.9 1.6 %collective-permute-start.4 = (bf16[384,1280]{1,0:T(8,128)(2,1)S(1)}, bf16[384,1280]{1,0:T(8,128)(2,1)S(1)}, u32[]{:S(2)}, u32[]{:S(2)}) collective-permute-start(bf16[384,1280]{1,0:T(8,128)(2,1)S(1)} %slice.83), channel_id=1, source_target_pairs={{0,64},{32,96},{64,0},{96,32},{1,65},{33,97},{65,1},{97,33},{2,66}... | collective-permute-start | bytes 2949128 | tf_op jit(solution)/shard_map/ppermute | solution.py:356
  14.6 2.7 %collective-permute-done.5.refs_2_.refs_3_ = bf16[1024,1152]{1,0:T(8,128)(2,1)S(1)} collective-permute-done((bf16[1024,1152]{1,0:T(8,128)(2,1)S(1)}, bf16[1024,1152]{1,0:T(8,128)(2,1)S(1)}, u32[]{:S(2)}, u32[]{:S(2)}) %collective-permute-start.5) | collective-permute-done | bytes 2359328 | tf_op jit(solution)/shard_map/ppermute | solution.py:364
  17.3 1.4 %copy-done.18 = bf16[1024,1152]{1,0:T(8,128)(2,1)} copy-done((bf16[1024,1152]{1,0:T(8,128)(2,1)}, bf16[1024,1152]{1,0:T(8,128)(2,1)S(1)}, u32[]{:S(2)}) %copy-start.18) | copy-done | bytes 2359320
  18.6 15.0 %adapt.3 = (bf16[1024,768]{1,0:T(8,128)(2,1)S(1)}, bf16[1024,1536]{1,0:T(8,128)(2,1)}, f32[1024,768]{1,0:T(8,128)}, f32[8,1024]{1,0:T(8,128)S(1)}, bf16[1024,768...) custom-call(bf16[512,1280]{1,0:T(8,128)(2,1)S(1)} %bitcast.26, ...), custom_call_target="tpu_custom_call" | custom-call | flops 1000 | bytes 1000 | tf_op jit(solution)/shard_map/adapt/pallas_call | solution.py:258
  33.6 1.2 copy-done.7
  34.9 1.2 copy-done.9
  37.3 1.0 copy-done.19
  38.3 7.8 %adapt.4 = (bf16[1024,768]{1,0:T(8,128)(2,1)}, bf16[1024,1536]{1,0:T(8,128)(2,1)}, f32[1024,768]{1,0:T(8,128)}, f32[8,1024]{1,0:T(8,128)}) custom-call(bf16[128,1280]{1,0:T(8,128)(2,1)} %copy-done.12, bf16[384,1280]{1,0:T(8,128)(2,1)} %copy-done.19, ...), custom_call_target="tpu_custom_call", output_to_operand_aliasing={{0}: (7, {}), {1}: (8, {}), {2}: (9, {}), {3}: (10, {})} | custom-call | flops 1000 | bytes 1000 | tf_op jit(solution)/shard_map/adapt/pallas_call | solution.py:258
  46.1 1.6 %collective-permute-start.6 = (f32[8,1024]{1,0:T(8,128)}, f32[8,1024]{1,0:T(8,128)S(1)}, u32[]{:S(2)}, u32[]{:S(2)}) collective-permute-start(f32[8,1024]{1,0:T(8,128)} %get-tuple-element.54), channel_id=1, source_target_pairs={{0,64},{32,96},{64,0},{96,32},{1,65},{33,97},{65,1},{97,33},{2,66}... | collective-permute-start | bytes 98312 | tf_op jit(solution)/shard_map/ppermute | solution.py:380
  47.7 11.2 %adapt.5 = (bf16[1024,768]{1,0:T(8,128)(2,1)}, bf16[1024,1280]{1,0:T(8,128)(2,1)}, f32[1024,768]{1,0:T(8,128)}, f32[8,1024]{1,0:T(8,128)S(1)}, bf16[1024,768]{1,...) custom-call(bf16[128,1280]{1,0:T(8,128)(2,1)S(1)} %copy-done.13, ...), custom_call_target="tpu_custom_call", output_to_operand_aliasing={{0}: (10, {}), {1}: (11, {}), {2}: (12, {}), {3}: (13, {}),... | custom-call | flops 1000 | bytes 1000 | tf_op jit(solution)/shard_map/adapt/pallas_call | solution.py:258
  59.6 1.5 %collective-permute-start.10 = (f32[8,1024]{1,0:T(8,128)S(1)}, f32[8,1024]{1,0:T(8,128)S(1)}, u32[]{:S(2)}, u32[]{:S(2)}) collective-permute-start(f32[8,1024]{1,0:T(8,128)S(1)} %get-tuple-element.76), channel_id=1, source_target_pairs={{0,64},{32,96},{64,0},{96,32},{1,65},{33,97},{65,1},{97,33},{2,66}... | collective-permute-start | bytes 98312 | tf_op jit(solution)/shard_map/ppermute | solution.py:380
  61.2 2.9 %convolution_convert_fusion.dino = bf16[1536,768]{1,0:T(8,128)(2,1)S(1)} fusion(bf16[1024,1536]{1,0:T(8,128)(2,1)S(1)} %copy-done.22, f32[1024,768]{1,0:T(8,128)S(1)} %copy-done.23, bf16[1024,768]{1,0:T(8,128)(2,1)S(1)} %copy-done.10, f32[1024]{0:T(1024)S(1)} %get-tuple-element.68, f32[1024]{0:T(1024)S(1)} %get-tuple-element.66), kind=kOutput, calls=%fused_computation | convolution fusion | flops 2421030912 | bytes 10231808 | tf_op jit(solution)/shard_map/tk,tc->kc/dot_general | solution.py:388
  64.5 2.5 %convolution_convert_fusion.2.sam = bf16[1280,768]{1,0:T(8,128)(2,1)S(1)} fusion(bf16[1024,1280]{1,0:T(8,128)(2,1)S(1)} %copy-done.24, f32[1024,768]{1,0:T(8,128)S(1)} %copy-done.20, bf16[1024,768]{1,0:T(8,128)(2,1)S(1)} %copy-done.8, f32[1024]{0:T(1024)S(1)} %get-tuple-element.73, f32[1024]{0:T(1024)S(1)} %get-tuple-element.71), kind=kOutput, calls=%fused_computation.2 | convolution fusion | flops 2018181120 | bytes 9314304 | tf_op jit(solution)/shard_map/tk,tc->kc/dot_general | solution.py:388
  67.7 2.3 %convolution_convert_fusion.1.siglip = bf16[1152,768]{1,0:T(8,128)(2,1)S(1)} fusion(bf16[1024,1152]{1,0:T(8,128)(2,1)S(1)} %copy-done.25, f32[1024,768]{1,0:T(8,128)S(1)} %copy-done.21, bf16[1024,768]{1,0:T(8,128)(2,1)S(1)} %copy-done.27, f32[1024]{0:T(1024)S(1)} %get-tuple-element.79, f32[1024]{0:T(1024)S(1)} %get-tuple-element.77), kind=kOutput, calls=%fused_computation.1 | convolution fusion | flops 1816756224 | bytes 8855552 | tf_op jit(solution)/shard_map/tk,tc->kc/dot_general | solution.py:388
  70.5 2.2 %collective-permute-done.11.siglip_other = bf16[1152,384]{1,0:T(8,128)(2,1)S(1)} collective-permute-done((bf16[1152,384]{1,0:T(8,128)(2,1)S(1)}, bf16[1152,384]{1,0:T(8,128)(2,1)S(1)}, u32[]{:S(2)}, u32[]{:S(2)}) %collective-permute-start.11) | collective-permute-done | bytes 884768 | tf_op jit(solution)/shard_map/ppermute | solution.py:397
  72.7 1.6 %pack.1 = bf16[32,336,128]{2,1,0:T(8,128)(2,1)S(1)} custom-call(bf16[1536,768]{1,0:T(8,128)(2,1)S(1)} %convolution_convert_fusion.dino, bf16[1536,384]{1,0:T(8,128)(2,1)S(1)} %collective-permute-done.7.dino_other, bf16[1280,768]{1,0:T(8,128)(2,1)S(1)} %convolution_convert_fusion.2.sam, bf16[1280,384]{1,0:T(8,128)(2,1)S(1)} %collective-permute-done.9.sam_other, ...), custom_call_target="tpu_custom_call" | custom-call | tf_op jit(solution)/shard_map/pack/pallas_call | solution.py:296
  74.3 47.4 %all_to_all.5.split = bf16[32,336,128]{2,1,0:T(8,128)(2,1)S(1)} all-to-all(bf16[32,336,128]{2,1,0:T(8,128)(2,1)S(1)} %pack.1), channel_id=1, replica_groups=mesh['grp'=4,'dp'=32] {'dp'}, dimensions={0} | all-to-all | bytes 5505024 | tf_op jit(solution)/shard_map/all_to_all | solution.py:398
  121.7 1.1 unpack.1
  (86 shorter events, 4.9 us)
Async XLA Ops:
  0.6 12.0 %collective-permute-start.1 = (bf16[1536,384]{1,0:T(8,128)(2,1)}, bf16[1536,384]{1,0:T(8,128)(2,1)S(1)}, u32[]{:S(2)}, u32[]{:S(2)}) collective-permute-start(bf16[1536,384]{1,0:T(8,128)(2,1)} %refs_5_.1), channel_id=1, source_target_pairs={{0,32},{32,0},{64,96},{96,64},{1,33},{33,1},{65,97},{97,65},{2,34}... | collective-permute-start | bytes 3538952 | tf_op jit(solution)/shard_map/ppermute | solution.py:359
  0.7 11.9 %collective-permute-start.2 = (bf16[320,1280]{1,0:T(8,128)(2,1)}, bf16[320,1280]{1,0:T(8,128)(2,1)}, u32[]{:S(2)}, u32[]{:S(2)}) collective-permute-start(bf16[320,1280]{1,0:T(8,128)(2,1)} %bitcast.27), channel_id=1, source_target_pairs={{0,32},{32,0},{64,96},{96,64},{1,33},{33,1},{65,97},{97,65},{2,34}... | collective-permute-start | bytes 2457608 | tf_op jit(solution)/shard_map/ppermute | solution.py:359
  1.2 11.4 %collective-permute-start.3 = (bf16[288,1152]{1,0:T(8,128)(2,1)}, bf16[288,1152]{1,0:T(8,128)(2,1)}, u32[]{:S(2)}, u32[]{:S(2)}) collective-permute-start(bf16[288,1152]{1,0:T(8,128)(2,1)} %bitcast.30), channel_id=1, source_target_pairs={{0,32},{32,0},{64,96},{96,64},{1,33},{33,1},{65,97},{97,65},{2,34}... | collective-permute-start | bytes 1990664 | tf_op jit(solution)/shard_map/ppermute | solution.py:359
  2.3 10.3 %collective-permute-start = (bf16[128,1280]{1,0:T(8,128)(2,1)S(1)}, bf16[128,1280]{1,0:T(8,128)(2,1)S(1)}, u32[]{:S(2)}, u32[]{:S(2)}) collective-permute-start(bf16[128,1280]{1,0:T(8,128)(2,1)S(1)} %slice.82), channel_id=1, source_target_pairs={{0,64},{32,96},{64,0},{96,32},{1,65},{33,97},{65,1},{97,33},{2,66}... | collective-permute-start | bytes 983048 | tf_op jit(solution)/shard_map/ppermute | solution.py:356
  7.6 11.0 %copy-start.2 = (bf16[1536,384]{1,0:T(8,128)(2,1)S(1)}, bf16[1536,384]{1,0:T(8,128)(2,1)}, u32[]{:S(2)}) copy-start(bf16[1536,384]{1,0:T(8,128)(2,1)} %refs_5_.1) | copy-start | bytes 3538948
  7.6 11.0 %copy-start.4 = (bf16[1280,320]{0,1:T(8,128)(2,1)S(1)}, bf16[1280,320]{0,1:T(8,128)(2,1)}, u32[]{:S(2)}) copy-start(bf16[1280,320]{0,1:T(8,128)(2,1)} %param.19) | copy-start | bytes 2457604
  7.6 11.0 %copy-start.6 = (bf16[1152,288]{0,1:T(8,128)(2,1)S(1)}, bf16[1152,288]{0,1:T(8,128)(2,1)}, u32[]{:S(2)}) copy-start(bf16[1152,288]{0,1:T(8,128)(2,1)} %param.17) | copy-start | bytes 1990660
  12.6 21.0 %copy-start.12 = (bf16[128,1280]{1,0:T(8,128)(2,1)}, bf16[128,1280]{1,0:T(8,128)(2,1)S(1)}, u32[]{:S(2)}) copy-start(bf16[128,1280]{1,0:T(8,128)(2,1)S(1)} %collective-permute-done.refs_0_) | copy-start | bytes 983044
  12.6 21.0 %copy-start.3 = (bf16[1536,384]{1,0:T(8,128)(2,1)}, bf16[1536,384]{1,0:T(8,128)(2,1)S(1)}, u32[]{:S(2)}) copy-start(bf16[1536,384]{1,0:T(8,128)(2,1)S(1)} %collective-permute-done.1.refs_5_.refs_6_) | copy-start | bytes 3538948
  12.6 4.6 %collective-permute-start.5 = (bf16[1024,1152]{1,0:T(8,128)(2,1)S(1)}, bf16[1024,1152]{1,0:T(8,128)(2,1)S(1)}, u32[]{:S(2)}, u32[]{:S(2)}) collective-permute-start(bf16[1024,1152]{1,0:T(8,128)(2,1)S(1)} %bitcast.33), channel_id=1, source_target_pairs={{0,32},{32,0},{64,96},{96,64},{1,33},{33,1},{65,97},{97,65},{2,34}... | collective-permute-start | bytes 7077896 | tf_op jit(solution)/shard_map/ppermute | solution.py:364
  12.9 24.3 %collective-permute-start.4 = (bf16[384,1280]{1,0:T(8,128)(2,1)S(1)}, bf16[384,1280]{1,0:T(8,128)(2,1)S(1)}, u32[]{:S(2)}, u32[]{:S(2)}) collective-permute-start(bf16[384,1280]{1,0:T(8,128)(2,1)S(1)} %slice.83), channel_id=1, source_target_pairs={{0,64},{32,96},{64,0},{96,32},{1,65},{33,97},{65,1},{97,33},{2,66}... | collective-permute-start | bytes 2949128 | tf_op jit(solution)/shard_map/ppermute | solution.py:356
  38.3 9.4 %copy-start.5 = (bf16[1280,320]{0,1:T(8,128)(2,1)S(1)}, bf16[1280,320]{0,1:T(8,128)(2,1)}, u32[]{:S(2)}) copy-start(bf16[1280,320]{0,1:T(8,128)(2,1)} %param.19) | copy-start | bytes 2457604
  38.3 9.4 %copy-start.13 = (bf16[128,1280]{1,0:T(8,128)(2,1)S(1)}, bf16[128,1280]{1,0:T(8,128)(2,1)}, u32[]{:S(2)}) copy-start(bf16[128,1280]{1,0:T(8,128)(2,1)} %copy-done.12) | copy-start | bytes 983044
  38.3 9.4 %copy-start.15 = (f32[8,1024]{1,0:T(8,128)S(1)}, f32[8,1024]{1,0:T(8,128)}, u32[]{:S(2)}) copy-start(f32[8,1024]{1,0:T(8,128)} %copy-done.14) | copy-start | bytes 98308
  46.1 15.0 %collective-permute-start.6 = (f32[8,1024]{1,0:T(8,128)}, f32[8,1024]{1,0:T(8,128)S(1)}, u32[]{:S(2)}, u32[]{:S(2)}) collective-permute-start(f32[8,1024]{1,0:T(8,128)} %get-tuple-element.54), channel_id=1, source_target_pairs={{0,64},{32,96},{64,0},{96,32},{1,65},{33,97},{65,1},{97,33},{2,66}... | collective-permute-start | bytes 98312 | tf_op jit(solution)/shard_map/ppermute | solution.py:380
  47.6 13.4 %copy-start.17 = (f32[8,1024]{1,0:T(8,128)S(1)}, f32[8,1024]{1,0:T(8,128)}, u32[]{:S(2)}) copy-start(f32[8,1024]{1,0:T(8,128)} %get-tuple-element.54) | copy-start | bytes 98308
  47.6 13.5 %copy-start.10 = (bf16[1024,768]{1,0:T(8,128)(2,1)S(1)}, bf16[1024,768]{1,0:T(8,128)(2,1)}, u32[]{:S(2)}) copy-start(bf16[1024,768]{1,0:T(8,128)(2,1)} %get-tuple-element.67) | copy-start | bytes 4718596
  47.7 13.5 %copy-start.22 = (bf16[1024,1536]{1,0:T(8,128)(2,1)S(1)}, bf16[1024,1536]{1,0:T(8,128)(2,1)}, u32[]{:S(2)}) copy-start(bf16[1024,1536]{1,0:T(8,128)(2,1)} %get-tuple-element.53) | copy-start | bytes 9437188
  47.7 13.5 %copy-start.23 = (f32[1024,768]{1,0:T(8,128)S(1)}, f32[1024,768]{1,0:T(8,128)}, u32[]{:S(2)}) copy-start(f32[1024,768]{1,0:T(8,128)} %get-tuple-element.69) | copy-start | bytes 9437188
  58.9 5.4 %collective-permute-start.8 = (f32[8,1024]{1,0:T(8,128)S(1)}, f32[8,1024]{1,0:T(8,128)S(1)}, u32[]{:S(2)}, u32[]{:S(2)}) collective-permute-start(f32[8,1024]{1,0:T(8,128)S(1)} %get-tuple-element.65), channel_id=1, source_target_pairs={{0,64},{32,96},{64,0},{96,32},{1,65},{33,97},{65,1},{97,33},{2,66}... | collective-permute-start | bytes 98312 | tf_op jit(solution)/shard_map/ppermute | solution.py:380
  59.6 8.1 %collective-permute-start.10 = (f32[8,1024]{1,0:T(8,128)S(1)}, f32[8,1024]{1,0:T(8,128)S(1)}, u32[]{:S(2)}, u32[]{:S(2)}) collective-permute-start(f32[8,1024]{1,0:T(8,128)S(1)} %get-tuple-element.76), channel_id=1, source_target_pairs={{0,64},{32,96},{64,0},{96,32},{1,65},{33,97},{65,1},{97,33},{2,66}... | collective-permute-start | bytes 98312 | tf_op jit(solution)/shard_map/ppermute | solution.py:380
  64.2 8.4 %collective-permute-start.7 = (bf16[1536,384]{1,0:T(8,128)(2,1)S(1)}, bf16[1536,384]{1,0:T(8,128)(2,1)S(1)}, u32[]{:S(2)}, u32[]{:S(2)}) collective-permute-start(bf16[1536,384]{1,0:T(8,128)(2,1)S(1)} %slice.89), channel_id=1, source_target_pairs={{0,32},{32,0},{64,96},{96,64},{1,33},{33,1},{65,97},{97,65},{2,34}... | collective-permute-start | bytes 3538952 | tf_op jit(solution)/shard_map/ppermute | solution.py:397
  67.1 5.6 %collective-permute-start.9 = (bf16[1280,384]{1,0:T(8,128)(2,1)S(1)}, bf16[1280,384]{1,0:T(8,128)(2,1)S(1)}, u32[]{:S(2)}, u32[]{:S(2)}) collective-permute-start(bf16[1280,384]{1,0:T(8,128)(2,1)S(1)} %slice.95), channel_id=1, source_target_pairs={{0,32},{32,0},{64,96},{96,64},{1,33},{33,1},{65,97},{97,65},{2,34}... | collective-permute-start | bytes 2949128 | tf_op jit(solution)/shard_map/ppermute | solution.py:397
  70.1 2.5 %collective-permute-start.11 = (bf16[1152,384]{1,0:T(8,128)(2,1)S(1)}, bf16[1152,384]{1,0:T(8,128)(2,1)S(1)}, u32[]{:S(2)}, u32[]{:S(2)}) collective-permute-start(bf16[1152,384]{1,0:T(8,128)(2,1)S(1)} %slice.101), channel_id=1, source_target_pairs={{0,32},{32,0},{64,96},{96,64},{1,33},{33,1},{65,97},{97,65},{2,34}... | collective-permute-start | bytes 2654216 | tf_op jit(solution)/shard_map/ppermute | solution.py:397
  (16 other events, 35.8 us)
